TPU v7x, 128 devices: a whole 4x4x4 slice. The times are simulated.
128 devices in a mesh: dp: 16 (over x, y_hi, core), tensor: 8 (over z, y_lo).
Axes of the slice: x: 4, y: 4 (y_hi: 2, y_lo: 2; y = y_hi * 2 + y_lo), z: 4, core: 2. Of those that a mesh axis runs over, the one named last changes fastest.
Arguments:
- stream: bfloat16 [8192, 4096], P(('dp', 'tensor')), may hold values from -16 to 16
- final_gain: float32 [4096], replicated, may hold values from 0.1 to 1.9
- residual: bfloat16 [8192, 4096], P(('dp', 'tensor')), may hold values from -16 to 16
- ffn_gain: float32 [4096], replicated, may hold values from 0.1 to 1.9
- queries: bfloat16 [4096, 2048], P('dp', 'tensor'), may hold values from -2 to 2
- saved_keys: bfloat16 [8192, 2048], P('dp', 'tensor'), may hold values from -1.75 to 1.75
- saved_values: bfloat16 [8192, 2048], P('dp', 'tensor'), may hold values from -6 to 6
- context_grad: bfloat16 [4096, 2048], P('dp', 'tensor'), may hold values from -24 to 24
- key_weight: bfloat16 [4096, 2048], P('dp', 'tensor'), may hold values from -0.09375 to 0.09375
- value_weight: bfloat16 [4096, 2048], P('dp', 'tensor'), may hold values from -0.09375 to 0.09375
- gate_weight: bfloat16 [4096, 8192], P(None, 'tensor'), may hold values from -0.09375 to 0.09375
- up_weight: bfloat16 [4096, 8192], P(None, 'tensor'), may hold values from -0.09375 to 0.09375
- down_weight: bfloat16 [8192, 4096], P('tensor', 'dp'), may hold values from -0.0625 to 0.0625
Outputs:
- residual_grad: bfloat16 [8192, 4096], P(('dp', 'tensor'))
- query_grad: bfloat16 [4096, 2048], P('dp', 'tensor')
- key_weight_grad: bfloat16 [4096, 2048], P('dp', 'tensor')
- value_weight_grad: bfloat16 [4096, 2048], P('dp', 'tensor')
All inputs are finite; a program needn't handle non-finite values.
Results may differ from a plain program's by a relative error of at most 0.03.
Values may be sent and summed in bfloat16 or wider, within the bound.
A program may use at most 192 MiB of HBM per device.

v0:
```python
import jax
import jax.numpy as jnp
from jax import lax
from jax.sharding import PartitionSpec as P

HEAD_DIM = 256


def rms_scale(values_wide):
    return lax.rsqrt(jnp.mean(values_wide * values_wide, axis=-1, keepdims=True) + 1e-06)


def norm_back(grad_in, values_wide, scale, gain):
    scaled = grad_in * gain
    return scale * scaled - values_wide * (scale * scale * scale) * jnp.mean(
        scaled * values_wide, axis=-1, keepdims=True
    )


def local(
    stream,
    final_gain,
    residual,
    ffn_gain,
    queries,
    saved_keys,
    saved_values,
    context_grad,
    key_weight,
    value_weight,
    gate_weight,
    up_weight,
    down_weight,
):
    own_rows = stream.shape[0]
    inner_here = saved_keys.shape[1]
    heads_here = inner_here // HEAD_DIM
    contract_rows = (((0,), (0,)), ((), ()))
    contract_cols = (((1,), (1,)), ((), ()))
    group_stream, group_resid = (
        lax.all_gather(stream, "tensor", axis=0, tiled=True),
        lax.all_gather(residual, "tensor", axis=0, tiled=True),
    )
    stream_wide = group_stream.astype(jnp.float32)
    enc_scale = rms_scale(stream_wide)
    enc_out = (stream_wide * enc_scale * final_gain).astype(jnp.bfloat16)
    resid_wide = group_resid.astype(jnp.float32)
    res_scale = rms_scale(resid_wide)
    ffn_in = (resid_wide * res_scale * ffn_gain).astype(jnp.bfloat16)
    full_key_weight, full_value_weight = (
        lax.all_gather(key_weight, "dp", axis=0, tiled=True),
        lax.all_gather(value_weight, "dp", axis=0, tiled=True),
    )
    query_heads = queries.reshape(queries.shape[0], heads_here, HEAD_DIM)
    key_heads = saved_keys.reshape(saved_keys.shape[0], heads_here, HEAD_DIM)
    value_heads = saved_values.reshape(saved_values.shape[0], heads_here, HEAD_DIM)
    out_grad = context_grad.reshape(context_grad.shape[0], heads_here, HEAD_DIM)
    scores = jnp.einsum("qhd,khd->hqk", query_heads, key_heads, preferred_element_type=jnp.float32)
    attn_probs = jax.nn.softmax(scores, axis=-1)
    probs_low = attn_probs.astype(jnp.bfloat16)
    prob_grad = jnp.einsum(
        "qhd,khd->hqk", out_grad, value_heads, preferred_element_type=jnp.float32
    )
    row_delta = jnp.sum(attn_probs * prob_grad, axis=-1, keepdims=True)
    score_grad = (attn_probs * (prob_grad - row_delta)).astype(jnp.bfloat16)
    value_grad = (
        jnp.einsum("hqk,qhd->khd", probs_low, out_grad, preferred_element_type=jnp.float32)
        .astype(jnp.bfloat16)
        .reshape(-1, inner_here)
    )
    key_grad = (
        jnp.einsum("hqk,qhd->khd", score_grad, query_heads, preferred_element_type=jnp.float32)
        .astype(jnp.bfloat16)
        .reshape(-1, inner_here)
    )
    query_grad = (
        jnp.einsum("hqk,khd->qhd", score_grad, key_heads, preferred_element_type=jnp.float32)
        .astype(jnp.bfloat16)
        .reshape(queries.shape)
    )
    paired_grad = jnp.concatenate([key_grad, value_grad], axis=1)
    local_sums = lax.dot_general(
        enc_out, paired_grad, contract_rows, preferred_element_type=jnp.float32
    )
    weight_sums = lax.psum_scatter(
        local_sums.astype(jnp.bfloat16), "dp", scatter_dimension=0, tiled=True
    ).astype(jnp.float32)
    key_weight_grad = weight_sums[:, :inner_here].astype(jnp.bfloat16)
    value_weight_grad = weight_sums[:, inner_here:].astype(jnp.bfloat16)
    gate_pre = jnp.dot(ffn_in, gate_weight, preferred_element_type=jnp.float32)
    up_pre = jnp.dot(ffn_in, up_weight, preferred_element_type=jnp.float32)
    first_row = lax.axis_index("tensor") * own_rows
    first = lax.dot_general(
        key_grad, full_key_weight, contract_cols, preferred_element_type=jnp.float32
    )
    enc_grad = lax.psum(
        (
            first
            + lax.dot_general(
                value_grad, full_value_weight, contract_cols, preferred_element_type=jnp.float32
            )
        ).astype(jnp.bfloat16),
        "tensor",
    ).astype(jnp.float32)
    stream_grad = norm_back(enc_grad, stream_wide, enc_scale, final_gain)
    own_grad = lax.dynamic_slice_in_dim(stream_grad, first_row, own_rows, 0)
    ffn_rows = stream_grad.astype(jnp.bfloat16)
    hidden_grad = lax.dot_general(
        ffn_rows,
        lax.all_gather(down_weight, "dp", axis=1, tiled=True),
        contract_cols,
        preferred_element_type=jnp.float32,
    )
    gate_sig = jax.nn.sigmoid(gate_pre)
    gate_grad = (hidden_grad * up_pre * gate_sig * (1.0 + gate_pre * (1.0 - gate_sig))).astype(
        jnp.bfloat16
    )
    up_grad = (hidden_grad * gate_pre * gate_sig).astype(jnp.bfloat16)
    first = lax.dot_general(
        gate_grad, gate_weight, contract_cols, preferred_element_type=jnp.float32
    )
    in_share = lax.psum_scatter(
        (
            first
            + lax.dot_general(up_grad, up_weight, contract_cols, preferred_element_type=jnp.float32)
        ).astype(jnp.bfloat16),
        "tensor",
        scatter_dimension=0,
        tiled=True,
    ).astype(jnp.float32)
    own_resid = lax.dynamic_slice_in_dim(resid_wide, first_row, own_rows, 0)
    own_res_scale = lax.dynamic_slice_in_dim(res_scale, first_row, own_rows, 0)
    residual_grad = (own_grad + norm_back(in_share, own_resid, own_res_scale, ffn_gain)).astype(
        jnp.bfloat16
    )
    return (residual_grad, query_grad, key_weight_grad, value_weight_grad)


def solution(mesh):
    return jax.shard_map(
        local,
        mesh=mesh,
        in_specs=(
            P(("dp", "tensor"), None),
            P(),
            P(("dp", "tensor"), None),
            P(),
            P("dp", "tensor"),
            P("dp", "tensor"),
            P("dp", "tensor"),
            P("dp", "tensor"),
            P("dp", "tensor"),
            P("dp", "tensor"),
            P(None, "tensor"),
            P(None, "tensor"),
            P("tensor", "dp"),
        ),
        out_specs=(
            P(("dp", "tensor"), None),
            P("dp", "tensor"),
            P("dp", "tensor"),
            P("dp", "tensor"),
        ),
        check_vma=False,
    )
```

profile of v0, /device:TPU:0, one launch (start us, length us, event | category | flops | bytes accessed | tf_op | source)
XLA Modules:
  0.0 749.0 jit_solution(16271416944604275284)
XLA Ops:
  7.2 0.7 all-gather.8.cloned.1.call-update
  8.0 0.7 all-gather.10.cloned.1.call-update
  8.7 0.7 all-gather.12.cloned.1.call-update
  9.4 0.5 all-gather.6.cloned.1.call-update
  10.0 1.2 fusion.24
  11.5 1.4 multiply_reduce_fusion.2
  13.1 1.2 convolution_convert_fusion.2
  14.3 1.3 convolution_convert_fusion.1
  15.6 45.7 %all-gather.8.cloned.1.call-done = bf16[4096,256]{1,0:T(8,128)(2,1)} async-done(((bf16[256,256]{1,0:T(8,128)(2,1)}), bf16[4096,256]{1,0:T(8,128)(2,1)}) %all-gather.8.cloned.1.call-update) | async-done | bytes 2097168 | tf_op jit(solution)/shard_map/all_gather | solution.py:51
  61.2 6.1 fusion.25
  67.4 43.5 %all-gather.10.cloned.1.call-done = bf16[4096,256]{1,0:T(8,128)(2,1)} async-done(((bf16[256,256]{1,0:T(8,128)(2,1)}), bf16[4096,256]{1,0:T(8,128)(2,1)}) %all-gather.10.cloned.1.call-update) | async-done | bytes 2097168 | tf_op jit(solution)/shard_map/all_gather | solution.py:52
  110.9 7.3 add_convert_fusion.1
  118.8 83.5 %all-gather.12.cloned.1.call-done = bf16[512,4096]{1,0:T(8,128)(2,1)} async-done(((bf16[64,4096]{1,0:T(8,128)(2,1)}), bf16[512,4096]{1,0:T(8,128)(2,1)}) %all-gather.12.cloned.1.call-update) | async-done | bytes 4194320 | tf_op jit(solution)/shard_map/all_gather | solution.py:42
  202.4 3.1 multiply_reduce_fusion
  205.5 8.3 %fusion.11 = f32[512,1024]{1,0:T(8,128)S(1)} fusion(bf16[4096,1024]{1,0:T(8,128)(2,1)} %param.23, f32[4096]{0:T(1024)S(1)} %copy-done.3, f32[512]{0:T(512)S(1)} %add_rsqrt_fusion, bf16[512,4096]{1,0:T(8,128)(2,1)} %all-gather.12.cloned.1.call-done), kind=kOutput, calls=%fused_computation.23 | convolution fusion | flops 4303355904 | bytes 14698496 | tf_op jit(solution)/shard_map/dot_general | solution.py:90
  213.7 80.9 %all-gather.6.cloned.1.call-done = bf16[512,4096]{1,0:T(8,128)(2,1)} async-done(((bf16[64,4096]{1,0:T(8,128)(2,1)}), bf16[512,4096]{1,0:T(8,128)(2,1)}) %all-gather.6.cloned.1.call-update) | async-done | bytes 4194320 | tf_op jit(solution)/shard_map/all_gather | solution.py:41
  294.6 185.2 %all-reduce.2.cloned.1.call-done = bf16[512,4096]{1,0:T(8,128)(2,1)} async-done(((bf16[512,4096]{1,0:T(8,128)(2,1)}), bf16[512,4096]{1,0:T(8,128)(2,1)}) %all-reduce.2.cloned.1.call-update) | async-done | bytes 4194320 | tf_op jit(solution)/shard_map/psum | solution.py:96
  479.9 4.7 fusion
  484.6 4.7 convolution_convert_fusion
  489.6 7.2 fusion.2
  496.7 65.2 %all-gather.14.cloned.1.call-done = bf16[1024,4096]{1,0:T(8,128)(2,1)} async-done(((bf16[1024,256]{1,0:T(8,128)(2,1)}), bf16[1024,4096]{1,0:T(8,128)(2,1)}) %all-gather.14.cloned.1.call-update) | async-done | bytes 8388624 | tf_op jit(solution)/shard_map/all_gather | solution.py:110
  561.9 11.8 %fusion.7 = f32[512,1024]{1,0:T(8,128)} fusion(bf16[1024,4096]{1,0:T(8,128)(2,1)} %all-gather.14.cloned.1.call-done, f32[512,4096]{1,0:T(8,128)} %fusion.2), kind=kOutput, calls=%fused_computation.16 | convolution fusion | flops 4297064448 | bytes 18874368 | tf_op jit(solution)/shard_map/dot_general | solution.py:108
  573.7 9.6 %multiply_convert_fusion.2 = bf16[512,1024]{1,0:T(8,128)(2,1)S(1)} fusion(f32[512,1024]{1,0:T(8,128)S(1)} %fusion.11, f32[512,1024]{1,0:T(8,128)} %fusion.7, bf16[4096,1024]{1,0:T(8,128)(2,1)} %param.24, f32[4096]{0:T(1024)S(1)} %copy-done.3, f32[512]{0:T(512)S(1)} %add_rsqrt_fusion, bf16[512,4096]{1,0:T(8,128)(2,1)S(1)} %copy-done.1), kind=kOutput, calls=%fused_computation.21 | convolution fusion | flops 4308598784 | bytes 17844224 | tf_op jit(solution)/shard_map/dot_general | solution.py:91
  583.3 6.8 fusion.26
  590.1 12.9 %add_convert_fusion = bf16[512,4096]{1,0:T(8,128)(2,1)} fusion(f32[512,4096]{1,0:T(8,128)} %fusion.26, bf16[4096,1024]{1,0:T(8,128)(2,1)} %param.24, f32[512,1024]{1,0:T(8,128)} %fusion.7, f32[512,1024]{1,0:T(8,128)S(1)} %fusion.11), kind=kOutput, calls=%fused_computation.10 | convolution fusion | flops 4302307328 | bytes 25165824 | tf_op jit(solution)/shard_map/dot_general | solution.py:125
  603.0 0.9 convolution_convert_fusion.3
  603.9 6.5 convert_element_type.75
  610.5 34.4 %reduce-scatter.5.cloned.1.call-done = bf16[256,512]{1,0:T(8,128)(2,1)} async-done(((bf16[4096,512]{1,0:T(8,128)(2,1)}), bf16[256,512]{1,0:T(8,128)(2,1)}) %reduce-scatter.5.cloned.1.call-update) | async-done | bytes 262160 | tf_op jit(solution)/shard_map/reduce_scatter | solution.py:85
  644.9 1.7 fusion.23
  646.6 91.2 %reduce-scatter.3.cloned.1.call-done = bf16[64,4096]{1,0:T(8,128)(2,1)} async-done(((bf16[512,4096]{1,0:T(8,128)(2,1)}), bf16[64,4096]{1,0:T(8,128)(2,1)}) %reduce-scatter.3.cloned.1.call-update) | async-done | bytes 524304 | tf_op jit(solution)/shard_map/reduce_scatter | solution.py:122
  737.7 1.6 multiply_reduce_fusion.1
  739.3 2.8 add_convert_fusion.2
  (34 shorter events, 1.6 us)
Async XLA Ops:
  7.2 2.9 copy-start
  7.2 54.0 %all-gather.8.cloned.1.call-start = ((), (), s32[]{:S(2)}) async-start(), calls=%async_computation.3 | async-start | bytes 2228224 | tf_op jit(solution)/shard_map/all_gather | solution.py:51
  7.9 102.9 %all-gather.10.cloned.1.call-start = ((), (), s32[]{:S(2)}) async-start(), calls=%async_computation.4 | async-start | bytes 2228224 | tf_op jit(solution)/shard_map/all_gather | solution.py:52
  8.7 193.7 %all-gather.12.cloned.1.call-start = ((), (), s32[]{:S(2)}) async-start(), calls=%async_computation.6 | async-start | bytes 4718592 | tf_op jit(solution)/shard_map/all_gather | solution.py:42
  9.4 285.2 %all-gather.6.cloned.1.call-start = ((), (), s32[]{:S(2)}) async-start(), calls=%async_computation.2 | async-start | bytes 4718592 | tf_op jit(solution)/shard_map/all_gather | solution.py:41
  10.0 469.9 %all-reduce.2.cloned.1.call-start = ((), (), s32[]{:S(2)}) async-start(), calls=%async_computation.5 | async-start | bytes 8388608 | tf_op jit(solution)/shard_map/psum | solution.py:96
  67.4 138.1 %copy-start.3 = (f32[4096]{0:T(1024)S(1)}, f32[4096]{0:T(1024)}, u32[]{:S(2)}) copy-start(f32[4096]{0:T(1024)} %param.16) | copy-start | bytes 49156
  118.2 443.7 %all-gather.14.cloned.1.call-start = ((), (), s32[]{:S(2)}) async-start(), calls=%async_computation.7 | async-start | bytes 8912896 | tf_op jit(solution)/shard_map/all_gather | solution.py:110
  118.8 526.1 %reduce-scatter.5.cloned.1.call-start = ((), (), s32[]{:S(2)}) async-start(), calls=%async_computation.9 | async-start | bytes 4456448 | tf_op jit(solution)/shard_map/reduce_scatter | solution.py:85
  205.5 274.4 %copy-start.4 = (f32[4096]{0:T(1024)S(1)}, f32[4096]{0:T(1024)}, u32[]{:S(2)}) copy-start(f32[4096]{0:T(1024)} %param.14) | copy-start | bytes 49156
  479.9 4.7 copy-start.2
  489.3 248.4 %reduce-scatter.3.cloned.1.call-start = ((), (), s32[]{:S(2)}) async-start(), calls=%async_computation.8 | async-start | bytes 4718592 | tf_op jit(solution)/shard_map/reduce_scatter | solution.py:122
  561.9 11.8 %copy-start.1 = (bf16[512,4096]{1,0:T(8,128)(2,1)S(1)}, bf16[512,4096]{1,0:T(8,128)(2,1)}, u32[]{:S(2)}) copy-start(bf16[512,4096]{1,0:T(8,128)(2,1)} %all-gather.12.cloned.1.call-done) | copy-start | bytes 12582916
  561.9 21.4 %slice-start = ((s8[8388608]{0:T(1024)(128)(4,1)}), s8[4194304]{0:T(1024)(128)(4,1)S(1)}, s32[]{:S(2)}) async-start(s8[8388608]{0:T(1024)(128)(4,1)} %bitcast.23), calls=%async_computation.10 | async-start | bytes 8388608
  573.7 9.6 %slice-start.1 = ((s8[8388608]{0:T(1024)(128)(4,1)}), s8[4194304]{0:T(1024)(128)(4,1)S(1)}, s32[]{:S(2)}) async-start(s8[8388608]{0:T(1024)(128)(4,1)} %bitcast.23), calls=%async_computation.11 | async-start | bytes 8388608
Sparse Core Ops, SparseCore 0:
  10.4 50.7 all-gather.7
  63.6 47.1 all-gather.9
  112.5 89.8 all-gather.11
  203.9 90.7 all-gather.5
  297.0 182.8 all-reduce.1
  482.0 79.8 all-gather.13
  566.0 78.8 reduce-scatter.4
  647.4 90.2 reduce-scatter.2
where the time goes:
time: 750 us; the launch traced here: 749 us
  waiting for transfers between devices  633 us (84%)
  matrix products  73.4 us (10%)
  other arithmetic  26.4 us (4%)
  between operations  14.3 us (2%)
    psum x1, waiting for transfers between devices, local(): lax.psum((first + lax.dot_general(value_grad, full_value_weight, contract...  185 us
    reduce_scatter x1, waiting for transfers between devices, local(): lax.psum_scatter((first + lax.dot_general(up_grad, up_weight, contract_co...  91.2 us
    all_gather x1, waiting for transfers between devices, local(): lax.all_gather(residual, 'tensor', axis=0, tiled=True)  83.5 us
    all_gather x1, waiting for transfers between devices, local(): lax.all_gather(stream, 'tensor', axis=0, tiled=True)  80.9 us
    all_gather x1, waiting for transfers between devices, local(): lax.all_gather(down_weight, 'dp', axis=1, tiled=True)  65.2 us
    all_gather x1, waiting for transfers between devices, local(): lax.all_gather(key_weight, 'dp', axis=0, tiled=True)  45.7 us
    all_gather x1, waiting for transfers between devices, local(): lax.all_gather(value_weight, 'dp', axis=0, tiled=True)  43.5 us
    reduce_scatter x1, waiting for transfers between devices, local(): lax.psum_scatter(local_sums.astype(jnp.bfloat16), 'dp', scatter_dimension...  34.4 us
  transfers between devices with their start and end apart: 8, of which 8 were waited for; matrix products, arithmetic and copies ran while one was open for 13% of the time, Pallas kernels for 0%

commit v1 on v0

v1 whole, which is shorter than its diff:
```python
import jax
import jax.numpy as jnp
from jax import lax
from jax.experimental import pallas as pl
from jax.experimental.pallas import tpu as pltpu
from jax.sharding import PartitionSpec as P

BF = jnp.bfloat16
F32 = jnp.float32
D, TOK, OWN, FFL, HD, Q = 4096, 512, 64, 1024, 256, 256
NCH, CW = 8, 512
WCH, WR = 4, 128

NN = (((1,), (0,)), ((), ()))
NT = (((1,), (1,)), ((), ()))
TN = (((0,), (0,)), ((), ()))


def dot(a, b, dims=NN):
    return lax.dot_general(a, b, dims, preferred_element_type=F32)


class Place:
    def __init__(self):
        dp, tn = lax.axis_index("dp"), lax.axis_index("tensor")
        self.dp, self.tn = dp, tn
        self.x, self.h, self.c = dp // 4, (dp // 2) % 2, dp % 2
        self.z, self.l = tn // 2, tn % 2
        self.xu, self.xd, self.x2 = (self.x + 1) % 4, (self.x + 3) % 4, (self.x + 2) % 4
        self.zu, self.zd, self.z2 = (self.z + 1) % 4, (self.z + 3) % 4, (self.z + 2) % 4


def dp_of(x, h, c):
    return (x * 2 + h) * 2 + c


def tn_of(z, l):
    return z * 2 + l


def remote(src, dst, ss, rs, dev):
    return pltpu.make_async_remote_copy(
        src_ref=src, dst_ref=dst, send_sem=ss, recv_sem=rs, device_id=dev,
        device_id_type=pl.DeviceIdType.MESH,
    )


class TensorGather:
    def __init__(self, p, buf, ss, rs):
        z, l, zu, zd, z2, m = p.z, p.l, p.zu, p.zd, p.z2, 1 - p.l
        up, dn, pair = {"tensor": tn_of(zu, l)}, {"tensor": tn_of(zd, l)}, {"tensor": tn_of(z, m)}
        self.buf, self.ss, self.rs = buf, ss, rs
        self.t = [
            ((z, l), (z, m), 0, OWN, pair),
            ((z, l), (zd, l), 0, OWN, up),
            ((z, l), (zu, l), 0, OWN, dn),
            ((z, m), (zd, m), 0, OWN, up),
            ((z, m), (zu, m), 0, OWN, dn),
            ((zd, l), (z2, l), 0, OWN // 2, up),
            ((zu, l), (z2, l), OWN // 2, OWN // 2, dn),
            ((zd, m), (z2, m), 0, OWN // 2, up),
            ((zu, m), (z2, m), OWN // 2, OWN // 2, dn),
        ]

    def _rows(self, shard, first, n):
        return self.buf.at[pl.ds(pl.multiple_of(tn_of(*shard) * OWN + first, 32), n)]

    def _copy(self, i, received):
        sent, got, first, n, to = self.t[i]
        ref = self._rows(got if received else sent, first, n)
        return remote(ref, ref, self.ss.at[i], self.rs.at[i], to)

    def send(self, *idx):
        for i in idx:
            self._copy(i, False).start()

    def recv(self, *idx):
        for i in idx:
            self._copy(i, True).wait_recv()

    def s0(self):
        self.send(0, 1, 2)

    def s1(self):
        self.recv(0)
        self.send(3, 4)

    def s2(self):
        self.recv(1)
        self.send(5)
        self.recv(2)
        self.send(6)

    def s3(self):
        self.recv(3)
        self.send(7)
        self.recv(4)
        self.send(8)

    def s4(self):
        self.recv(5, 6, 7, 8)

    def drain(self):
        for i in range(9):
            self._copy(i, False).wait_send()


class DpGather:
    def __init__(self, p, buf, ss, rs, rows):
        x, h, c, xu, xd, x2, o, g = p.x, p.h, p.c, p.xu, p.xd, p.x2, 1 - p.h, 1 - p.c
        up, dn = {"dp": dp_of(xu, h, c)}, {"dp": dp_of(xd, h, c)}
        pair, core = {"dp": dp_of(x, o, c)}, {"dp": dp_of(x, h, g)}
        self.buf, self.ss, self.rs = buf, ss, rs
        r, hf = rows, rows // 2
        self.t = [
            ((x, h, c), (x, h, g), 0, r, core),
            ((x, h, c), (x, o, c), 0, r, pair),
            ((x, h, c), (xd, h, c), 0, r, up),
            ((x, h, c), (xu, h, c), 0, r, dn),
            ((x, o, c), (xd, o, c), 0, r, up),
            ((x, o, c), (xu, o, c), 0, r, dn),
            ((xd, h, c), (x2, h, c), 0, hf, up),
            ((xu, h, c), (x2, h, c), hf, hf, dn),
            ((xd, o, c), (x2, o, c), 0, hf, up),
            ((xu, o, c), (x2, o, c), hf, hf, dn),
            ((x, o, c), (x, o, g), 0, r, core),
            ((xd, h, c), (xd, h, g), 0, r, core),
            ((xu, h, c), (xu, h, g), 0, r, core),
            ((xd, o, c), (xd, o, g), 0, r, core),
            ((xu, o, c), (xu, o, g), 0, r, core),
            ((x2, h, c), (x2, h, g), 0, r, core),
            ((x2, o, c), (x2, o, g), 0, r, core),
        ]

    def _copy(self, i, received, src=None):
        sent, got, first, n, to = self.t[i]
        sx, sh, sc = got if received else sent
        ref = self.buf.at[sc, sx * 2 + sh, pl.ds(first, n)]
        return remote(ref if src is None else src, ref, self.ss.at[i], self.rs.at[i], to)

    def send(self, *idx, src=None):
        for i in idx:
            self._copy(i, False, src).start()

    def recv(self, *idx):
        for i in idx:
            self._copy(i, True).wait_recv()

    def s0(self, src=None):
        self.send(1, 2, 3, 0, src=src)

    def step(self, k):
        if k == 0:
            self.recv(0)
        elif k < 6:
            self.recv(k)
            if k == 1:
                self.send(4, 5, 10)
            else:
                self.send(k + 4, k + 9)
            self.recv(k + 9)
        elif k == 6:
            self.recv(6, 7)
            self.send(15)
            self.recv(15)
        else:
            self.recv(8, 9)
            self.send(16)
            self.recv(16)

    def drain(self):
        for i in range(17):
            self._copy(i, False).wait_send()


class RingReduce:
    def __init__(self, part, far, near, ysend, yrecv, ss, rs, ring, pair, up, dn, mate):
        self.part, self.far, self.near, self.ysend, self.yrecv = part, far, near, ysend, yrecv
        self.ss, self.rs = ss, rs
        self.r, self.ru, self.rd, self.r2 = ring
        self.l, self.m = pair, 1 - pair
        self.up, self.dn, self.mate = up, dn, mate

    def _copy(self, i, k):
        p = self.part(k)
        src, dst, to = [
            (lambda: p.at[self.r2 * 2], lambda: self.far.at[k, 0], self.up),
            (lambda: p.at[self.r2 * 2 + 1], lambda: self.far.at[k, 1], self.dn),
            (lambda: p.at[self.ru * 2 + 1], lambda: self.near.at[k, 1], self.up),
            (lambda: p.at[self.rd * 2], lambda: self.near.at[k, 2], self.dn),
            (lambda: p.at[self.ru * 2], lambda: self.near.at[k, 0], self.up),
            (lambda: p.at[self.rd * 2 + 1], lambda: self.near.at[k, 3], self.dn),
            (lambda: self.ysend.at[k], lambda: self.yrecv.at[k], self.mate),
        ][i]
        return remote(src(), dst(), self.ss.at[k, i], self.rs.at[k, i], to)

    def stage1(self, k):
        for i in range(4):
            self._copy(i, k).start()

    def stage2(self, k):
        p = self.part(k)
        for i, blk in ((0, self.ru * 2), (1, self.rd * 2 + 1)):
            self._copy(i, k).wait_recv()
            p[blk] = (p[blk].astype(F32) + self.far[k, i].astype(F32)).astype(BF)
            self._copy(4 + i, k).start()

    def stage3(self, k):
        for i in (2, 3, 4, 5):
            self._copy(i, k).wait_recv()
        p = self.part(k)

        def total(pair):
            return (
                p[self.r * 2 + pair].astype(F32)
                + self.near[k, pair].astype(F32)
                + self.near[k, 2 + pair].astype(F32)
            )

        self.ysend[k] = total(self.m).astype(BF)
        self._copy(6, k).start()
        return total(self.l)

    def stage4(self, k):
        self._copy(6, k).wait_recv()
        return self.yrecv[k].astype(F32)

    def drain(self, n):
        def body(k, _):
            for i in range(7):
                self._copy(i, k).wait_send()
            return 0

        lax.fori_loop(0, n, body, 0)


def kernel(
    stream, final_gain, residual, ffn_gain, queries, keys, values, ctx, key_w, value_w,
    gate_hbm, up_hbm, down_hbm,
    out_ref, qg_ref, kwg_ref, vwg_ref, down_all,
    res_g, str_g, ffn_g, kvw, gate_v, up_v, down_v, part, far, near, ysend, yrecv,
    coef_a, coef_b, ggrad, ugrad, acc, sgrad, kvg, kvg_t,
    crecv, wfar, wnear, wysend, wyrecv, wacc,
    res_ss, res_rs, str_ss, str_rs, ffn_ss, ffn_rs, kv_ss, kv_rs, dn_ss, dn_rs,
    er_ss, er_rs, ir_ss, ir_rs, wr_ss, wr_rs, cs_ss, cs_rs, loc, dsem,
):
    p = Place()
    MESH = pl.DeviceIdType.MESH
    z_up, z_dn = {"tensor": tn_of(p.zu, p.l)}, {"tensor": tn_of(p.zd, p.l)}
    mate = {"tensor": tn_of(p.z, 1 - p.l)}
    x_up, x_dn = {"dp": dp_of(p.xu, p.h, p.c)}, {"dp": dp_of(p.xd, p.h, p.c)}
    h_mate, core = {"dp": dp_of(p.x, 1 - p.h, p.c)}, {"dp": dp_of(p.x, p.h, 1 - p.c)}

    barrier = pltpu.get_barrier_semaphore()
    for dev in (z_up, z_dn, mate, x_up, x_dn, h_mate, core):
        pl.semaphore_signal(barrier, inc=1, device_id=dev, device_id_type=MESH)

    own_chip = p.x * 2 + p.h
    gate_load = pltpu.make_async_copy(gate_hbm, gate_v, loc.at[0])
    up_load = pltpu.make_async_copy(up_hbm, up_v, loc.at[1])
    down_own = pltpu.make_async_copy(down_hbm, down_all.at[p.c, own_chip], loc.at[2])
    down_own.start()
    gate_load.start()
    up_load.start()

    kvw[p.c, own_chip, 0:HD, :] = key_w[...]
    kvw[p.c, own_chip, HD : 2 * HD, :] = value_w[...]
    own = pl.multiple_of(p.tn * OWN, OWN)

    def normed(src, gain, dst):
        def body(i, _):
            r = pl.multiple_of(i * 16, 16)
            v = src[pl.ds(r, 16), :].astype(F32)
            s = lax.rsqrt(jnp.mean(v * v, axis=-1, keepdims=True) + 1e-06)
            dst[pl.ds(pl.multiple_of(own + r, 16), 16), :] = (v * s * gain[...]).astype(BF)
            return 0

        lax.fori_loop(0, OWN // 16, body, 0)

    kv = DpGather(p, kvw, kv_ss, kv_rs, 2 * HD)
    down = DpGather(p, down_all, dn_ss, dn_rs, FFL)
    res = TensorGather(p, res_g, res_ss, res_rs)
    stm = TensorGather(p, str_g, str_ss, str_rs)
    ffn = TensorGather(p, ffn_g, ffn_ss, ffn_rs)

    pl.semaphore_wait(barrier, 7)
    kv.s0()
    normed(residual, ffn_gain, res_g)
    res.s0()
    normed(stream, final_gain, str_g)
    stm.s0()

    s_t = dot(keys[...], queries[...], NT)
    e_t = jnp.exp(s_t - jnp.max(s_t, axis=0, keepdims=True))
    probs = e_t / jnp.sum(e_t, axis=0, keepdims=True)
    pg = dot(values[...], ctx[...], NT)
    delta = jnp.sum(probs * pg, axis=0, keepdims=True)
    sg = (probs * (pg - delta)).astype(BF)
    vgrad = dot(probs.astype(BF), ctx[...])
    kgrad = dot(sg, queries[...])
    kvg[:, 0:HD] = kgrad.astype(BF)
    kvg[:, HD : 2 * HD] = vgrad.astype(BF)
    kvg_t[0:HD, :] = kgrad.T.astype(BF)
    kvg_t[HD : 2 * HD, :] = vgrad.T.astype(BF)
    qg_ref[...] = dot(sg, keys[...], TN).astype(BF)

    ring_z = (p.z, p.zu, p.zd, p.z2)
    ring_x = (p.x, p.xu, p.xd, p.x2)
    enc_rs = RingReduce(
        lambda k: part.at[k], far, near, ysend, yrecv, er_ss, er_rs, ring_z, p.l, z_up, z_dn, mate
    )
    in_rs = RingReduce(
        lambda k: part.at[k], far, near, ysend, yrecv, ir_ss, ir_rs, ring_z, p.l, z_up, z_dn, mate
    )
    w_rs = RingReduce(
        lambda k: kvw.at[p.c, :, pl.ds(pl.multiple_of(k * WR, WR), WR), :],
        wfar, wnear, wysend, wyrecv, wr_ss, wr_rs, ring_x, p.h, x_up, x_dn, h_mate,
    )

    def chunk_of(k):
        if isinstance(k, int):
            return [
                p.x * 2 + p.h, p.x * 2 + 1 - p.h, p.xd * 2 + p.h, p.xu * 2 + p.h,
                p.xd * 2 + 1 - p.h, p.xu * 2 + 1 - p.h, p.x2 * 2 + p.h, p.x2 * 2 + 1 - p.h,
            ][k]
        raise TypeError

    def enc_compute(k):
        chip = chunk_of(k)
        for cc in range(2):
            blk = dot(kvg[:, 0:HD], kvw[cc, chip, 0:HD, :], NT)
            blk = blk + dot(kvg[:, HD : 2 * HD], kvw[cc, chip, HD : 2 * HD, :], NT)
            part[k, :, :, cc * HD : (cc + 1) * HD] = blk.astype(BF).reshape(8, OWN, HD)

    services = {
        1: [res.s1],
        2: [res.s2],
        4: [stm.s1],
        5: [res.s3],
        6: [stm.s2],
        8: [stm.s3],
    }
    for k in range(NCH + 3):
        if k < NCH:
            kv.step(k)
            enc_compute(k)
            enc_rs.stage1(k)
        for service in services.get(k, []):
            service()
        if k == 4:
            down_own.wait()
            down.s0()
        if 0 <= k - 1 < NCH:
            enc_rs.stage2(k - 1)
        if 0 <= k - 2 < NCH:
            acc[k - 2] = enc_rs.stage3(k - 2)
        if 0 <= k - 3 < NCH:
            acc[k - 3] = acc[k - 3] + enc_rs.stage4(k - 3)

    def cols(k):
        start = chunk_of(k) * CW
        return pl.ds(pl.multiple_of(start, CW), CW)

    sq = jnp.zeros((OWN, 1), F32)
    ip = jnp.zeros((OWN, 1), F32)
    for k in range(NCH):
        v = stream[:, cols(k)].astype(F32)
        sq = sq + jnp.sum(v * v, axis=-1, keepdims=True)
        ip = ip + jnp.sum(acc[k] * final_gain[:, cols(k)] * v, axis=-1, keepdims=True)
    scale = lax.rsqrt(sq * (1.0 / D) + 1e-06)
    mix = scale * scale * scale * (ip * (1.0 / D))
    for k in range(NCH):
        v = stream[:, cols(k)].astype(F32)
        grad = scale * (acc[k] * final_gain[:, cols(k)]) - v * mix
        sgrad[:, cols(k)] = grad
        ffn_g[pl.ds(own, OWN), cols(k)] = grad.astype(BF)
    ffn.s0()

    gate_load.wait()
    up_load.wait()
    down.step(0)
    down.step(1)
    res.s4()

    def gate_tile(j):
        c0 = pl.ds(pl.multiple_of(j * HD, HD), HD)
        gate = dot(res_g[...], gate_v[:, c0])
        up = dot(res_g[...], up_v[:, c0])
        sig = 1.0 / (1.0 + jnp.exp(-gate))
        coef_a[:, c0] = (up * sig * (1.0 + gate * (1.0 - sig))).astype(BF)
        coef_b[:, c0] = (gate * sig).astype(BF)

    def gate_tiles(lo, hi):
        lax.fori_loop(lo, hi, lambda j, _: (gate_tile(j), 0)[1], 0)

    gate_tiles(0, 2)
    down.step(2)
    down.step(3)
    ffn.s1()
    gate_tiles(2, 4)
    down.step(4)
    down.step(5)
    ffn.s2()
    stm.s4()
    kv.drain()

    def w_tile(chip, _):
        for cc in range(2):
            c0 = pl.ds(pl.multiple_of((chip * 2 + cc) * HD, HD), HD)
            kvw[cc, chip] = dot(kvg_t[...], str_g[:, c0]).astype(BF)
        return 0

    lax.fori_loop(0, 8, w_tile, 0)
    down.step(6)
    down.step(7)

    def down_load(j):
        s = j % 2
        return pltpu.make_async_copy(
            down_all.at[:, :, pl.ds(pl.multiple_of(j * HD, HD), HD), :], down_v.at[s], dsem.at[s]
        )

    down_load(0).start()
    ffn.s3()

    def core_copy(k):
        rows = pl.ds(pl.multiple_of(k * WR, WR), WR)
        return remote(
            kvw.at[1 - p.c, :, rows, :], crecv.at[k], cs_ss.at[k], cs_rs.at[k], core
        )

    for k in range(WCH):
        core_copy(k).start()
    enc_rs.drain(NCH)
    ffn.s4()

    def hidden_tile(j, _):
        @pl.when(j < 3)
        def _():
            down_load(j + 1).start()

        down_load(j).wait()
        s = j % 2
        hid = jnp.zeros((TOK, HD), F32)
        for i in range(16):
            hid = hid + dot(ffn_g[:, i * HD : (i + 1) * HD], down_v[s, i % 2, i // 2], NT)
        c0 = pl.ds(pl.multiple_of(j * HD, HD), HD)
        ggrad[:, c0] = (hid * coef_a[:, c0].astype(F32)).astype(BF)
        ugrad[:, c0] = (hid * coef_b[:, c0].astype(F32)).astype(BF)
        return 0

    lax.fori_loop(0, 4, hidden_tile, 0)

    def in_step(k, _):
        @pl.when(k < NCH)
        def _():
            rows = pl.ds(pl.multiple_of(k * CW, CW), CW)
            blk = dot(ggrad[...], gate_v[rows, :], NT) + dot(ugrad[...], up_v[rows, :], NT)
            part[k] = blk.astype(BF).reshape(8, OWN, CW)
            in_rs.stage1(k)

        @pl.when(k < WCH)
        def _():
            core_copy(k).wait_recv()
            mine = w_rs.part(k)
            mine[...] = (mine[...].astype(F32) + crecv[k].astype(F32)).astype(BF)
            w_rs.stage1(k)

        @pl.when((k >= 1) & (k < NCH + 1))
        def _():
            in_rs.stage2(k - 1)

        @pl.when((k >= 1) & (k < WCH + 1))
        def _():
            w_rs.stage2(k - 1)

        @pl.when((k >= 2) & (k < NCH + 2))
        def _():
            acc[k - 2] = in_rs.stage3(k - 2)

        @pl.when((k >= 2) & (k < WCH + 2))
        def _():
            wacc[k - 2] = w_rs.stage3(k - 2)

        @pl.when(k >= 3)
        def _():
            acc[k - 3] = acc[k - 3] + in_rs.stage4(k - 3)

        @pl.when((k >= 3) & (k < WCH + 3))
        def _():
            wacc[k - 3] = wacc[k - 3] + w_rs.stage4(k - 3)

        return 0

    lax.fori_loop(0, NCH + 3, in_step, 0)

    for half in range(2):
        kwg_ref[:, half * WR : (half + 1) * WR] = wacc[half].T.astype(BF)
        vwg_ref[:, half * WR : (half + 1) * WR] = wacc[2 + half].T.astype(BF)

    sq = jnp.zeros((OWN, 1), F32)
    ip = jnp.zeros((OWN, 1), F32)
    for k in range(NCH):
        c0 = slice(k * CW, (k + 1) * CW)
        v = residual[:, c0].astype(F32)
        sq = sq + jnp.sum(v * v, axis=-1, keepdims=True)
        ip = ip + jnp.sum(acc[k] * ffn_gain[:, c0] * v, axis=-1, keepdims=True)
    scale = lax.rsqrt(sq * (1.0 / D) + 1e-06)
    mix = scale * scale * scale * (ip * (1.0 / D))
    for k in range(NCH):
        c0 = slice(k * CW, (k + 1) * CW)
        v = residual[:, c0].astype(F32)
        out_ref[:, c0] = (
            sgrad[:, c0] + scale * (acc[k] * ffn_gain[:, c0]) - v * mix
        ).astype(BF)

    for g in (res, stm, ffn, down):
        g.drain()
    in_rs.drain(NCH)
    w_rs.drain(WCH)
    for k in range(WCH):
        core_copy(k).wait_send()


def local(
    stream, final_gain, residual, ffn_gain, queries, saved_keys, saved_values, context_grad,
    key_weight, value_weight, gate_weight, up_weight, down_weight,
):
    vm = pl.BlockSpec(memory_space=pltpu.VMEM)
    hbm = pl.BlockSpec(memory_space=pl.ANY)
    dma = pltpu.SemaphoreType.DMA
    sds = jax.ShapeDtypeStruct
    v = pltpu.VMEM
    outs = pl.pallas_call(
        kernel,
        out_shape=(
            sds((OWN, D), BF), sds((Q, HD), BF), sds((HD, HD), BF), sds((HD, HD), BF),
            sds((2, 8, FFL, HD), BF),
        ),
        in_specs=[vm] * 10 + [hbm] * 3,
        out_specs=(vm, vm, vm, vm, hbm),
        scratch_shapes=[
            v((TOK, D), BF), v((TOK, D), BF), v((TOK, D), BF),
            v((2, 8, 2 * HD, HD), BF),
            v((D, FFL), BF), v((D, FFL), BF),
            v((2, 2, 8, HD, HD), BF),
            v((NCH, 8, OWN, CW), BF),
            v((NCH, 2, OWN, CW), BF), v((NCH, 4, OWN, CW), BF),
            v((NCH, OWN, CW), BF), v((NCH, OWN, CW), BF),
            v((TOK, FFL), BF), v((TOK, FFL), BF), v((TOK, FFL), BF), v((TOK, FFL), BF),
            v((NCH, OWN, CW), F32), v((OWN, D), F32),
            v((TOK, 2 * HD), BF), v((2 * HD, TOK), BF),
            v((WCH, 8, WR, HD), BF),
            v((WCH, 2, WR, HD), BF), v((WCH, 4, WR, HD), BF),
            v((WCH, WR, HD), BF), v((WCH, WR, HD), BF), v((WCH, WR, HD), F32),
            dma((9,)), dma((9,)), dma((9,)), dma((9,)), dma((9,)), dma((9,)),
            dma((17,)), dma((17,)), dma((17,)), dma((17,)),
            dma((NCH, 7)), dma((NCH, 7)), dma((NCH, 7)), dma((NCH, 7)),
            dma((WCH, 7)), dma((WCH, 7)), dma((WCH,)), dma((WCH,)),
            dma((3,)), dma((2,)),
        ],
        compiler_params=pltpu.CompilerParams(
            collective_id=0, has_side_effects=True, vmem_limit_bytes=64 * 1024 * 1024
        ),
        name="cross_ffn_backward",
    )(
        stream, final_gain.reshape(1, D), residual, ffn_gain.reshape(1, D), queries, saved_keys,
        saved_values, context_grad, key_weight, value_weight, gate_weight, up_weight, down_weight,
    )
    return outs[:4]


def solution(mesh):
    return jax.shard_map(
        local,
        mesh=mesh,
        in_specs=(
            P(("dp", "tensor"), None), P(), P(("dp", "tensor"), None), P(),
            P("dp", "tensor"), P("dp", "tensor"), P("dp", "tensor"), P("dp", "tensor"),
            P("dp", "tensor"), P("dp", "tensor"), P(None, "tensor"), P(None, "tensor"),
            P("tensor", "dp"),
        ),
        out_specs=(
            P(("dp", "tensor"), None), P("dp", "tensor"), P("dp", "tensor"), P("dp", "tensor"),
        ),
        check_vma=False,
    )
```

time: 750 us -> 214 us (0.29)
  waiting for transfers between devices: 633 us -> 0 us
  Pallas kernels: 0 us -> 207 us
  matrix products: 73.4 us -> 0 us
  other arithmetic: 26.4 us -> 0 us
  between operations: 14.3 us -> 0.65 us
    all_gather x5 -> x0, waiting for transfers between devices: 319 us -> none  [the longest x1 83.5 us: local(): lax.all_gather(residual, 'tensor', axis=0, tiled=True)]
    pallas_call x0 -> x1, Pallas kernels: none -> 207 us  [local(): pl.pallas_call(kernel, out_shape=(sds((OWN, D), BF), sds((Q, HD), BF), sd...]
    psum x1 -> x0, waiting for transfers between devices: 185 us -> none  [local(): lax.psum((first + lax.dot_general(value_grad, full_value_weight, contract...]
    reduce_scatter x2 -> x0, waiting for transfers between devices: 126 us -> none  [the longest x1 91.2 us: local(): lax.psum_scatter((first + lax.dot_general(up_grad, up_weight, contract_co...]
    dot_general x13 -> x0, matrix products: 73.4 us -> none  [the longest x1 12.9 us: local(): lax.dot_general(up_grad, up_weight, contract_cols, preferred_element_type...]
    reduce_sum x4 -> x0, other arithmetic: 9.61 us -> none  [the longest x2 7.75 us: rms_scale(): jnp.mean(values_wide * values_wide, axis=-1, keepdims=True) + 1e-06]
    convert_element_type x3 -> x0, other arithmetic: 9.51 us -> none  [the longest x1 6.5 us: local(): resid_wide = group_resid.astype(jnp.float32)]
  transfers between devices with their start and end apart: 8 -> 0, of which waited for: 8 -> 0; matrix products, arithmetic and copies ran while one was open for 13% -> 0% of each run, Pallas kernels for 0% -> 0%
where the time goes in v1:
time: 214 us
  Pallas kernels  207 us (97%)
  local copies, waits for them, and re-layouts  6.57 us (3%)
    pallas_call x1, Pallas kernels, local(): pl.pallas_call(kernel, out_shape=(sds((OWN, D), BF), sds((Q, HD), BF), sd...  207 us
    unnamed x4, local copies, waits for them, and re-layouts  6.57 us

profile of v1, /device:TPU:0, one launch (start us, length us, event | category | flops | bytes accessed | tf_op | source)
XLA Modules:
  0.0 213.9 jit_solution(12522186396654551152)
XLA Ops:
  0.6 206.7 %cross_ffn_backward.1 = (bf16[64,4096]{1,0:T(8,128)(2,1)}, bf16[256,256]{1,0:T(8,128)(2,1)}, bf16[256,256]{1,0:T(8,128)(2,1)}, bf16[256,256]{1,0:T(8,128)(2,1)}, bf16[2,8,1024,256]{3,2,1,0:T(8,128)(2,1)}) custom-call(bf16[64,4096]{1,0:T(8,128)(2,1)} %stream.1, f32[1,4096]{1,0:T(1,128)} %bitcast.2, bf16[64,4096]{1,0:T(8,128)(2,1)} %residual.1, ...), custom_call_target="tpu_custom_call" | custom-call | tf_op jit(solution)/shard_map/cross_ffn_backward/pallas_call | solution.py:534
  207.4 1.9 copy.21
  209.2 1.6 copy.22
  210.8 1.6 copy.23
  212.4 1.6 copy.24

commit v2 on v1

--- a/solution.py
+++ b/solution.py
@@ -10,6 +10,7 @@
 D, TOK, OWN, FFL, HD, Q = 4096, 512, 64, 1024, 256, 256
 NCH, CW = 8, 512
 WCH, WR = 4, 128
+W0 = 4
 
 NN = (((1,), (0,)), ((), ()))
 NT = (((1,), (1,)), ((), ()))
@@ -102,6 +103,72 @@
 
     def drain(self):
         for i in range(9):
+            self._copy(i, False).wait_send()
+
+
+class ColumnGather:
+    def __init__(self, p, buf, ss, rs, up, dn, mate_a, mate_b):
+        z, zu, zd, z2 = p.z, p.zu, p.zd, p.z2
+        self.buf, self.ss, self.rs = buf, ss, rs
+        a, b = (4, mate_a), (6, mate_b)
+        self.t = [
+            (z, 0, zd, up), (z, 1, zu, dn), (z, 1, zd, up), (z, 0, zu, dn),
+            (z, 0, z, a), (z, 1, z, b),
+            (zd, 0, z2, up), (zd, 0, zd, a),
+            (zu, 1, z2, dn), (zu, 1, zu, b),
+            (zd, 1, zd, b), (zu, 0, zu, a),
+            (z2, 0, z2, a), (z2, 1, z2, b),
+        ]
+
+    def _rows(self, first):
+        return self.buf.at[pl.ds(pl.multiple_of(first, 32), 32)]
+
+    def _copy(self, i, received):
+        sent, half, got, to = self.t[i]
+        if isinstance(to, tuple):
+            base, dev = to
+            dst = self._rows(base * OWN + got * 32)
+            src = dst if received else self._rows(sent * OWN + half * 32)
+        else:
+            dev = to
+            dst = self._rows((got if received else sent) * OWN + half * 32)
+            src = dst
+        return remote(src, dst, self.ss.at[i], self.rs.at[i], dev)
+
+    def send(self, *idx):
+        for i in idx:
+            self._copy(i, False).start()
+
+    def recv(self, *idx):
+        for i in idx:
+            self._copy(i, True).wait_recv()
+
+    def s0(self):
+        self.send(0, 1, 4, 5, 2, 3)
+
+    def s1(self):
+        self.recv(0)
+        self.send(6, 7)
+        self.recv(1)
+        self.send(8, 9)
+
+    def s2(self):
+        self.recv(2)
+        self.send(10)
+        self.recv(3)
+        self.send(11)
+
+    def s3(self):
+        self.recv(6)
+        self.send(12)
+        self.recv(8)
+        self.send(13)
+
+    def s4(self):
+        self.recv(4, 5, 7, 9, 10, 11, 12, 13)
+
+    def drain(self):
+        for i in range(14):
             self._copy(i, False).wait_send()
 
 
@@ -149,24 +216,24 @@
     def s0(self, src=None):
         self.send(1, 2, 3, 0, src=src)
 
-    def step(self, k):
-        if k == 0:
-            self.recv(0)
-        elif k < 6:
-            self.recv(k)
-            if k == 1:
-                self.send(4, 5, 10)
+    def fwd(self, *ks):
+        for k in ks:
+            if k < 6:
+                self.recv(k)
+                if k == 1:
+                    self.send(4, 5, 10)
+                else:
+                    self.send(k + 4, k + 9)
+            elif k == 6:
+                self.recv(6, 7)
+                self.send(15)
             else:
-                self.send(k + 4, k + 9)
-            self.recv(k + 9)
-        elif k == 6:
-            self.recv(6, 7)
-            self.send(15)
-            self.recv(15)
-        else:
-            self.recv(8, 9)
-            self.send(16)
-            self.recv(16)
+                self.recv(8, 9)
+                self.send(16)
+
+    def done(self, *ks):
+        for k in ks:
+            self.recv(k + 9 if k else 0)
 
     def drain(self):
         for i in range(17):
@@ -234,12 +301,76 @@
         lax.fori_loop(0, n, body, 0)
 
 
+class ColumnReduce:
+    def __init__(self, p, part, near, far, side, ss, rs, up, dn, mate_a, mate_b):
+        self.z, self.zu, self.zd, self.z2 = p.z, p.zu, p.zd, p.z2
+        self.part, self.near, self.far, self.side = part, near, far, side
+        self.ss, self.rs = ss, rs
+        self.up, self.dn, self.a, self.b = up, dn, mate_a, mate_b
+
+    def _copy(self, i, k):
+        lo, hi = pl.ds(0, 32), pl.ds(32, 32)
+        src, dst, to = [
+            (lambda: self.part.at[k, pl.ds(4, 2)], lambda: self.side.at[k, pl.ds(0, 2)], self.a),
+            (lambda: self.part.at[k, pl.ds(6, 2)], lambda: self.side.at[k, pl.ds(2, 2)], self.b),
+            (lambda: self.part.at[k, self.z2, lo], lambda: self.far.at[k, 0, lo], self.up),
+            (lambda: self.part.at[k, self.z2, hi], lambda: self.far.at[k, 1, lo], self.dn),
+            (lambda: self.part.at[k, self.zu, hi], lambda: self.near.at[k, 0, hi], self.up),
+            (lambda: self.part.at[k, self.zd, lo], lambda: self.near.at[k, 1, lo], self.dn),
+            (lambda: self.part.at[k, self.zu, lo], lambda: self.near.at[k, 0, lo], self.up),
+            (lambda: self.part.at[k, self.zd, hi], lambda: self.near.at[k, 1, hi], self.dn),
+        ][i]
+        return remote(src(), dst(), self.ss.at[k, i], self.rs.at[k, i], to)
+
+    def stage1(self, k):
+        self._copy(0, k).start()
+        self._copy(1, k).start()
+
+    def stage2(self, k):
+        for i in range(2):
+            self._copy(i, k).wait_recv()
+            rows = pl.ds(32 * i, 32)
+            for zz in range(4):
+                got = self.side[k, 2 * i + zz // 2, pl.ds(32 * (zz % 2), 32)]
+                self.part[k, zz, rows] = (
+                    self.part[k, zz, rows].astype(F32) + got.astype(F32)
+                ).astype(BF)
+        for i in range(2, 6):
+            self._copy(i, k).start()
+
+    def stage3(self, k):
+        for i, blk in ((0, self.zu), (1, self.zd)):
+            self._copy(2 + i, k).wait_recv()
+            rows = pl.ds(32 * i, 32)
+            self.part[k, blk, rows] = (
+                self.part[k, blk, rows].astype(F32) + self.far[k, i, pl.ds(0, 32)].astype(F32)
+            ).astype(BF)
+            self._copy(6 + i, k).start()
+
+    def stage4(self, k):
+        for i in range(4, 8):
+            self._copy(i, k).wait_recv()
+        return (
+            self.part[k, self.z].astype(F32)
+            + self.near[k, 0].astype(F32)
+            + self.near[k, 1].astype(F32)
+        )
+
+    def drain(self, n):
+        def body(k, _):
+            for i in range(8):
+                self._copy(i, k).wait_send()
+            return 0
+
+        lax.fori_loop(0, n, body, 0)
+
+
 def kernel(
     stream, final_gain, residual, ffn_gain, queries, keys, values, ctx, key_w, value_w,
     gate_hbm, up_hbm, down_hbm,
     out_ref, qg_ref, kwg_ref, vwg_ref, down_all,
     res_g, str_g, ffn_g, kvw, gate_v, up_v, down_v, part, far, near, ysend, yrecv,
-    coef_a, coef_b, ggrad, ugrad, acc, sgrad, kvg, kvg_t,
+    inear, coef_a, coef_b, ggrad, ugrad, acc, sgrad, kvg, kvg_t,
     crecv, wfar, wnear, wysend, wyrecv, wacc,
     res_ss, res_rs, str_ss, str_rs, ffn_ss, ffn_rs, kv_ss, kv_rs, dn_ss, dn_rs,
     er_ss, er_rs, ir_ss, ir_rs, wr_ss, wr_rs, cs_ss, cs_rs, loc, dsem,
@@ -249,46 +380,48 @@
     z_up, z_dn = {"tensor": tn_of(p.zu, p.l)}, {"tensor": tn_of(p.zd, p.l)}
     mate = {"tensor": tn_of(p.z, 1 - p.l)}
     x_up, x_dn = {"dp": dp_of(p.xu, p.h, p.c)}, {"dp": dp_of(p.xd, p.h, p.c)}
+    mate_b = {"dp": dp_of(p.x, 1 - p.h, p.c), "tensor": tn_of(p.z, 1 - p.l)}
     h_mate, core = {"dp": dp_of(p.x, 1 - p.h, p.c)}, {"dp": dp_of(p.x, p.h, 1 - p.c)}
 
     barrier = pltpu.get_barrier_semaphore()
-    for dev in (z_up, z_dn, mate, x_up, x_dn, h_mate, core):
+    for dev in (z_up, z_dn, mate, mate_b, x_up, x_dn, h_mate, core):
         pl.semaphore_signal(barrier, inc=1, device_id=dev, device_id_type=MESH)
 
     own_chip = p.x * 2 + p.h
     gate_load = pltpu.make_async_copy(gate_hbm, gate_v, loc.at[0])
     up_load = pltpu.make_async_copy(up_hbm, up_v, loc.at[1])
-    down_own = pltpu.make_async_copy(down_hbm, down_all.at[p.c, own_chip], loc.at[2])
-    down_own.start()
+    down_in = pltpu.make_async_copy(down_hbm, crecv.at[0], loc.at[2])
+    down_in.start()
+    down_own = pltpu.make_async_copy(crecv.at[0], down_all.at[p.c, own_chip], loc.at[3])
     gate_load.start()
     up_load.start()
 
     kvw[p.c, own_chip, 0:HD, :] = key_w[...]
     kvw[p.c, own_chip, HD : 2 * HD, :] = value_w[...]
     own = pl.multiple_of(p.tn * OWN, OWN)
-
-    def normed(src, gain, dst):
+    own_z = pl.multiple_of(p.z * OWN, OWN)
+
+    def normed(src, gain, dst, at):
         def body(i, _):
             r = pl.multiple_of(i * 16, 16)
             v = src[pl.ds(r, 16), :].astype(F32)
             s = lax.rsqrt(jnp.mean(v * v, axis=-1, keepdims=True) + 1e-06)
-            dst[pl.ds(pl.multiple_of(own + r, 16), 16), :] = (v * s * gain[...]).astype(BF)
+            dst[pl.ds(pl.multiple_of(at + r, 16), 16), :] = (v * s * gain[...]).astype(BF)
             return 0
 
         lax.fori_loop(0, OWN // 16, body, 0)
 
     kv = DpGather(p, kvw, kv_ss, kv_rs, 2 * HD)
-    down = DpGather(p, down_all, dn_ss, dn_rs, FFL)
-    res = TensorGather(p, res_g, res_ss, res_rs)
+    down = DpGather(p, down_all, dn_ss, dn_rs, FFL // WR)
+    res = ColumnGather(p, res_g, res_ss, res_rs, z_up, z_dn, mate, mate_b)
     stm = TensorGather(p, str_g, str_ss, str_rs)
-    ffn = TensorGather(p, ffn_g, ffn_ss, ffn_rs)
-
-    pl.semaphore_wait(barrier, 7)
+    ffn = ColumnGather(p, ffn_g, ffn_ss, ffn_rs, z_up, z_dn, mate, mate_b)
+
+    pl.semaphore_wait(barrier, 8)
     kv.s0()
-    normed(residual, ffn_gain, res_g)
+    normed(residual, ffn_gain, res_g, own_z)
     res.s0()
-    normed(stream, final_gain, str_g)
-    stm.s0()
+    normed(stream, final_gain, str_g, own)
 
     s_t = dot(keys[...], queries[...], NT)
     e_t = jnp.exp(s_t - jnp.max(s_t, axis=0, keepdims=True))
@@ -304,13 +437,16 @@
     kvg_t[HD : 2 * HD, :] = vgrad.T.astype(BF)
     qg_ref[...] = dot(sg, keys[...], TN).astype(BF)
 
+    down_in.wait()
+    down_own.start()
+
     ring_z = (p.z, p.zu, p.zd, p.z2)
     ring_x = (p.x, p.xu, p.xd, p.x2)
     enc_rs = RingReduce(
         lambda k: part.at[k], far, near, ysend, yrecv, er_ss, er_rs, ring_z, p.l, z_up, z_dn, mate
     )
-    in_rs = RingReduce(
-        lambda k: part.at[k], far, near, ysend, yrecv, ir_ss, ir_rs, ring_z, p.l, z_up, z_dn, mate
+    in_rs = ColumnReduce(
+        p, part, inear, far, near, ir_ss, ir_rs, z_up, z_dn, mate, mate_b
     )
     w_rs = RingReduce(
         lambda k: kvw.at[p.c, :, pl.ds(pl.multiple_of(k * WR, WR), WR), :],
@@ -325,6 +461,10 @@
             ][k]
         raise TypeError
 
+    def start_down():
+        down_own.wait()
+        down.s0()
+
     def enc_compute(k):
         chip = chunk_of(k)
         for cc in range(2):
@@ -332,30 +472,37 @@
             blk = blk + dot(kvg[:, HD : 2 * HD], kvw[cc, chip, HD : 2 * HD, :], NT)
             part[k, :, :, cc * HD : (cc + 1) * HD] = blk.astype(BF).reshape(8, OWN, HD)
 
-    services = {
-        1: [res.s1],
-        2: [res.s2],
-        4: [stm.s1],
-        5: [res.s3],
-        6: [stm.s2],
-        8: [stm.s3],
+    lag = 4
+    before = {
+        1: lambda: kv.fwd(1),
+        2: lambda: kv.fwd(2, 3),
+        4: lambda: kv.fwd(4, 5),
+        6: lambda: kv.fwd(6),
+        7: lambda: kv.fwd(7),
     }
-    for k in range(NCH + 3):
+    after = {
+        2: res.s1,
+        4: start_down,
+        5: res.s2,
+        7: res.s3,
+        9: lambda: down.fwd(1),
+        11: lambda: down.fwd(2, 3),
+    }
+    for k in range(NCH + 2 + lag):
+        if k in before:
+            before[k]()
         if k < NCH:
-            kv.step(k)
+            kv.done(k)
             enc_compute(k)
             enc_rs.stage1(k)
-        for service in services.get(k, []):
-            service()
-        if k == 4:
-            down_own.wait()
-            down.s0()
-        if 0 <= k - 1 < NCH:
-            enc_rs.stage2(k - 1)
-        if 0 <= k - 2 < NCH:
-            acc[k - 2] = enc_rs.stage3(k - 2)
-        if 0 <= k - 3 < NCH:
-            acc[k - 3] = acc[k - 3] + enc_rs.stage4(k - 3)
+        if k in after:
+            after[k]()
+        if 0 <= k - lag < NCH:
+            enc_rs.stage2(k - lag)
+        if 0 <= k - lag - 1 < NCH:
+            acc[k - lag - 1] = enc_rs.stage3(k - lag - 1)
+        if 0 <= k - lag - 2 < NCH:
+            acc[k - lag - 2] = acc[k - lag - 2] + enc_rs.stage4(k - lag - 2)
 
     def cols(k):
         start = chunk_of(k) * CW
@@ -373,13 +520,11 @@
         v = stream[:, cols(k)].astype(F32)
         grad = scale * (acc[k] * final_gain[:, cols(k)]) - v * mix
         sgrad[:, cols(k)] = grad
-        ffn_g[pl.ds(own, OWN), cols(k)] = grad.astype(BF)
+        ffn_g[pl.ds(own_z, OWN), cols(k)] = grad.astype(BF)
     ffn.s0()
 
     gate_load.wait()
     up_load.wait()
-    down.step(0)
-    down.step(1)
     res.s4()
 
     def gate_tile(j):
@@ -393,16 +538,18 @@
     def gate_tiles(lo, hi):
         lax.fori_loop(lo, hi, lambda j, _: (gate_tile(j), 0)[1], 0)
 
-    gate_tiles(0, 2)
-    down.step(2)
-    down.step(3)
+    gate_tiles(0, 1)
+    down.fwd(4, 5)
     ffn.s1()
-    gate_tiles(2, 4)
-    down.step(4)
-    down.step(5)
+    stm.s0()
+    gate_tiles(1, 2)
     ffn.s2()
-    stm.s4()
-    kv.drain()
+    gate_tiles(2, 3)
+    down.fwd(6, 7)
+    ffn.s3()
+    stm.s1()
+    gate_tiles(3, 4)
+    down.done(*range(8))
 
     def w_tile(chip, _):
         for cc in range(2):
@@ -410,18 +557,13 @@
             kvw[cc, chip] = dot(kvg_t[...], str_g[:, c0]).astype(BF)
         return 0
 
-    lax.fori_loop(0, 8, w_tile, 0)
-    down.step(6)
-    down.step(7)
-
     def down_load(j):
         s = j % 2
         return pltpu.make_async_copy(
-            down_all.at[:, :, pl.ds(pl.multiple_of(j * HD, HD), HD), :], down_v.at[s], dsem.at[s]
+            down_all.at[:, :, pl.ds(j * 2, 2)], down_v.at[s], dsem.at[s]
         )
 
     down_load(0).start()
-    ffn.s3()
 
     def core_copy(k):
         rows = pl.ds(pl.multiple_of(k * WR, WR), WR)
@@ -429,9 +571,9 @@
             kvw.at[1 - p.c, :, rows, :], crecv.at[k], cs_ss.at[k], cs_rs.at[k], core
         )
 
-    for k in range(WCH):
-        core_copy(k).start()
     enc_rs.drain(NCH)
+    kv.drain()
+    stm.s2()
     ffn.s4()
 
     def hidden_tile(j, _):
@@ -443,7 +585,7 @@
         s = j % 2
         hid = jnp.zeros((TOK, HD), F32)
         for i in range(16):
-            hid = hid + dot(ffn_g[:, i * HD : (i + 1) * HD], down_v[s, i % 2, i // 2], NT)
+            hid = hid + dot(ffn_g[:, i * HD : (i + 1) * HD], down_v[s, i % 2, i // 2].reshape(HD, HD), NT)
         c0 = pl.ds(pl.multiple_of(j * HD, HD), HD)
         ggrad[:, c0] = (hid * coef_a[:, c0].astype(F32)).astype(BF)
         ugrad[:, c0] = (hid * coef_b[:, c0].astype(F32)).astype(BF)
@@ -459,40 +601,53 @@
             part[k] = blk.astype(BF).reshape(8, OWN, CW)
             in_rs.stage1(k)
 
-        @pl.when(k < WCH)
-        def _():
-            core_copy(k).wait_recv()
-            mine = w_rs.part(k)
-            mine[...] = (mine[...].astype(F32) + crecv[k].astype(F32)).astype(BF)
-            w_rs.stage1(k)
+        @pl.when(k == 1)
+        def _():
+            stm.s3()
+
+        @pl.when(k == W0)
+        def _():
+            stm.s4()
+            lax.fori_loop(0, 8, w_tile, 0)
+            for i in range(WCH):
+                core_copy(i).start()
+
+        w = k - W0 - 1
+
+        @pl.when((w >= 0) & (w < WCH))
+        def _():
+            core_copy(w).wait_recv()
+            mine = w_rs.part(w)
+            mine[...] = (mine[...].astype(F32) + crecv[w].astype(F32)).astype(BF)
+            w_rs.stage1(w)
 
         @pl.when((k >= 1) & (k < NCH + 1))
         def _():
             in_rs.stage2(k - 1)
 
-        @pl.when((k >= 1) & (k < WCH + 1))
-        def _():
-            w_rs.stage2(k - 1)
+        @pl.when((w >= 1) & (w < WCH + 1))
+        def _():
+            w_rs.stage2(w - 1)
 
         @pl.when((k >= 2) & (k < NCH + 2))
         def _():
-            acc[k - 2] = in_rs.stage3(k - 2)
-
-        @pl.when((k >= 2) & (k < WCH + 2))
-        def _():
-            wacc[k - 2] = w_rs.stage3(k - 2)
-
-        @pl.when(k >= 3)
-        def _():
-            acc[k - 3] = acc[k - 3] + in_rs.stage4(k - 3)
-
-        @pl.when((k >= 3) & (k < WCH + 3))
-        def _():
-            wacc[k - 3] = wacc[k - 3] + w_rs.stage4(k - 3)
+            in_rs.stage3(k - 2)
+
+        @pl.when((w >= 2) & (w < WCH + 2))
+        def _():
+            wacc[w - 2] = w_rs.stage3(w - 2)
+
+        @pl.when((k >= 3) & (k < NCH + 3))
+        def _():
+            acc[k - 3] = in_rs.stage4(k - 3)
+
+        @pl.when((w >= 3) & (w < WCH + 3))
+        def _():
+            wacc[w - 3] = wacc[w - 3] + w_rs.stage4(w - 3)
 
         return 0
 
-    lax.fori_loop(0, NCH + 3, in_step, 0)
+    lax.fori_loop(0, max(NCH + 3, W0 + WCH + 4), in_step, 0)
 
     for half in range(2):
         kwg_ref[:, half * WR : (half + 1) * WR] = wacc[half].T.astype(BF)
@@ -522,6 +677,11 @@
         core_copy(k).wait_send()
 
 
+def place_results(*refs):
+    for src, dst in zip(refs[:4], refs[4:]):
+        dst[...] = src[...]
+
+
 def local(
     stream, final_gain, residual, ffn_gain, queries, saved_keys, saved_values, context_grad,
     key_weight, value_weight, gate_weight, up_weight, down_weight,
@@ -535,7 +695,7 @@
         kernel,
         out_shape=(
             sds((OWN, D), BF), sds((Q, HD), BF), sds((HD, HD), BF), sds((HD, HD), BF),
-            sds((2, 8, FFL, HD), BF),
+            sds((2, 8, FFL // WR, WR, HD), BF),
         ),
         in_specs=[vm] * 10 + [hbm] * 3,
         out_specs=(vm, vm, vm, vm, hbm),
@@ -543,21 +703,22 @@
             v((TOK, D), BF), v((TOK, D), BF), v((TOK, D), BF),
             v((2, 8, 2 * HD, HD), BF),
             v((D, FFL), BF), v((D, FFL), BF),
-            v((2, 2, 8, HD, HD), BF),
+            v((2, 2, 8, 2, WR, HD), BF),
             v((NCH, 8, OWN, CW), BF),
             v((NCH, 2, OWN, CW), BF), v((NCH, 4, OWN, CW), BF),
             v((NCH, OWN, CW), BF), v((NCH, OWN, CW), BF),
+            v((NCH, 2, OWN, CW), BF),
             v((TOK, FFL), BF), v((TOK, FFL), BF), v((TOK, FFL), BF), v((TOK, FFL), BF),
             v((NCH, OWN, CW), F32), v((OWN, D), F32),
             v((TOK, 2 * HD), BF), v((2 * HD, TOK), BF),
             v((WCH, 8, WR, HD), BF),
             v((WCH, 2, WR, HD), BF), v((WCH, 4, WR, HD), BF),
             v((WCH, WR, HD), BF), v((WCH, WR, HD), BF), v((WCH, WR, HD), F32),
-            dma((9,)), dma((9,)), dma((9,)), dma((9,)), dma((9,)), dma((9,)),
+            dma((14,)), dma((14,)), dma((9,)), dma((9,)), dma((14,)), dma((14,)),
             dma((17,)), dma((17,)), dma((17,)), dma((17,)),
-            dma((NCH, 7)), dma((NCH, 7)), dma((NCH, 7)), dma((NCH, 7)),
+            dma((NCH, 7)), dma((NCH, 7)), dma((NCH, 8)), dma((NCH, 8)),
             dma((WCH, 7)), dma((WCH, 7)), dma((WCH,)), dma((WCH,)),
-            dma((3,)), dma((2,)),
+            dma((4,)), dma((2,)),
         ],
         compiler_params=pltpu.CompilerParams(
             collective_id=0, has_side_effects=True, vmem_limit_bytes=64 * 1024 * 1024
@@ -565,9 +726,16 @@
         name="cross_ffn_backward",
     )(
         stream, final_gain.reshape(1, D), residual, ffn_gain.reshape(1, D), queries, saved_keys,
-        saved_values, context_grad, key_weight, value_weight, gate_weight, up_weight, down_weight,
+        saved_values, context_grad, key_weight, value_weight, gate_weight, up_weight,
+        down_weight.reshape(FFL // WR, WR, HD),
     )
-    return outs[:4]
+    return pl.pallas_call(
+        place_results,
+        out_shape=tuple(sds(o.shape, o.dtype) for o in outs[:4]),
+        in_specs=[vm] * 4,
+        out_specs=(vm,) * 4,
+        name="place_results",
+    )(*outs[:4])
 
 
 def solution(mesh):

time: 214 us -> 167 us (0.78)
  Pallas kernels: 207 us -> 166 us
  local copies, waits for them, and re-layouts: 6.57 us -> 0 us
    pallas_call x1, Pallas kernels: 207 us -> 164 us  [local(): pl.pallas_call(kernel, out_shape=(sds((OWN, D), BF), sds((Q, HD), BF), sd...]
    unnamed x4 -> x0, local copies, waits for them, and re-layouts: 6.57 us -> none
where the time goes in v2:
time: 167 us; the launch traced here: 166 us
  Pallas kernels  166 us (99%)
    pallas_call x1, Pallas kernels, local(): pl.pallas_call(kernel, out_shape=(sds((OWN, D), BF), sds((Q, HD), BF), sd...  164 us

profile of v2, /device:TPU:0, one launch (start us, length us, event | category | flops | bytes accessed | tf_op | source)
XLA Modules:
  0.0 166.3 jit_solution(1067942284798135316)
XLA Ops:
  0.6 163.6 %cross_ffn_backward.1 = (bf16[64,4096]{1,0:T(8,128)(2,1)}, bf16[256,256]{1,0:T(8,128)(2,1)}, bf16[256,256]{1,0:T(8,128)(2,1)}, bf16[256,256]{1,0:T(8,128)(2,1)}, bf16[2,8,8,128,256]{4,3,2,1,0:T(8,128)(2,1)}) custom-call(bf16[64,4096]{1,0:T(8,128)(2,1)} %stream.1, f32[1,4096]{1,0:T(1,128)} %bitcast.4, bf16[64,4096]{1,0:T(8,128)(2,1)} %residual.1, ...), custom_call_target="tpu_custom_call" | custom-call | tf_op jit(solution)/shard_map/cross_ffn_backward/pallas_call | solution.py:694
  164.2 2.1 %place_results.1 = (bf16[64,4096]{1,0:T(8,128)(2,1)}, bf16[256,256]{1,0:T(8,128)(2,1)}, bf16[256,256]{1,0:T(8,128)(2,1)}, bf16[256,256]{1,0:T(8,128)(2,1)}) custom-call(bf16[64,4096]{1,0:T(8,128)(2,1)} %get-tuple-element.8.refs_0_, bf16[256,256]{1,0:T(8,128)(2,1)} %get-tuple-element.9.refs_1_, bf16[256,256]{1,0:T(8,128)(2,1)} %get-tuple-element.10.refs_2_, ...), custom_call_target="tpu_custom_call" | custom-call | tf_op jit(solution)/shard_map/place_results/pallas_call | solution.py:732

commit v3 on v2

--- a/solution.py
+++ b/solution.py
@@ -9,8 +9,14 @@
 F32 = jnp.float32
 D, TOK, OWN, FFL, HD, Q = 4096, 512, 64, 1024, 256, 256
 NCH, CW = 8, 512
+TH = TOK // 2
+NQ = 2 * NCH
+HALF, QTR = OWN // 2, OWN // 4
 WCH, WR = 4, 128
-W0 = 4
+ARRIVAL = (0, 2, 3, 6, 1, 4, 5, 7)
+LE, LI, LW = 5, 6, 4
+S2, S3 = 2, 6
+W0 = 11
 
 NN = (((1,), (0,)), ((), ()))
 NT = (((1,), (1,)), ((), ()))
@@ -52,24 +58,22 @@
         up, dn, pair = {"tensor": tn_of(zu, l)}, {"tensor": tn_of(zd, l)}, {"tensor": tn_of(z, m)}
         self.buf, self.ss, self.rs = buf, ss, rs
         self.t = [
-            ((z, l), (z, m), 0, OWN, pair),
-            ((z, l), (zd, l), 0, OWN, up),
-            ((z, l), (zu, l), 0, OWN, dn),
-            ((z, m), (zd, m), 0, OWN, up),
-            ((z, m), (zu, m), 0, OWN, dn),
-            ((zd, l), (z2, l), 0, OWN // 2, up),
-            ((zu, l), (z2, l), OWN // 2, OWN // 2, dn),
-            ((zd, m), (z2, m), 0, OWN // 2, up),
-            ((zu, m), (z2, m), OWN // 2, OWN // 2, dn),
+            ((z, l), (z, m), 0, 64, pair),
+            ((z, l), (zd, l), 0, 64, up),
+            ((z, l), (zu, l), 0, 64, dn),
+            ((z, m), (zd, m), 0, 64, up),
+            ((z, m), (zu, m), 0, 64, dn),
+            ((zd, l), (z2, l), 0, 32, up),
+            ((zu, l), (z2, l), 32, 32, dn),
+            ((zd, m), (z2, m), 0, 32, up),
+            ((zu, m), (z2, m), 32, 32, dn),
         ]
-
-    def _rows(self, shard, first, n):
-        return self.buf.at[pl.ds(pl.multiple_of(tn_of(*shard) * OWN + first, 32), n)]
 
     def _copy(self, i, received):
         sent, got, first, n, to = self.t[i]
-        ref = self._rows(got if received else sent, first, n)
-        return remote(ref, ref, self.ss.at[i], self.rs.at[i], to)
+        at = tn_of(*(got if received else sent)) * OWN + first
+        ref = self.buf.at[pl.ds(pl.multiple_of(at, 16), n)]
+        return remote(ref, ref, self.ss, self.rs.at[i], to)
 
     def send(self, *idx):
         for i in idx:
@@ -80,7 +84,7 @@
             self._copy(i, True).wait_recv()
 
     def s0(self):
-        self.send(0, 1, 2)
+        self.send(1, 2, 0)
 
     def s1(self):
         self.recv(0)
@@ -102,14 +106,14 @@
         self.recv(5, 6, 7, 8)
 
     def drain(self):
-        for i in range(9):
-            self._copy(i, False).wait_send()
+        sent = self.buf.at[pl.ds(0, 448)]
+        remote(sent, sent, self.ss, self.rs.at[0], self.t[0][4]).wait_send()
 
 
 class ColumnGather:
-    def __init__(self, p, buf, ss, rs, up, dn, mate_a, mate_b):
+    def __init__(self, p, buf, base, ss, rs, up, dn, mate_a, mate_b):
         z, zu, zd, z2 = p.z, p.zu, p.zd, p.z2
-        self.buf, self.ss, self.rs = buf, ss, rs
+        self.buf, self.base, self.ss, self.rs = buf, base, ss, rs
         a, b = (4, mate_a), (6, mate_b)
         self.t = [
             (z, 0, zd, up), (z, 1, zu, dn), (z, 1, zd, up), (z, 0, zu, dn),
@@ -121,19 +125,19 @@
         ]
 
     def _rows(self, first):
-        return self.buf.at[pl.ds(pl.multiple_of(first, 32), 32)]
+        return self.buf.at[pl.ds(pl.multiple_of(self.base + first, 16), QTR)]
 
     def _copy(self, i, received):
         sent, half, got, to = self.t[i]
         if isinstance(to, tuple):
             base, dev = to
-            dst = self._rows(base * OWN + got * 32)
-            src = dst if received else self._rows(sent * OWN + half * 32)
+            dst = self._rows(base * HALF + got * QTR)
+            src = dst if received else self._rows(sent * HALF + half * QTR)
         else:
             dev = to
-            dst = self._rows((got if received else sent) * OWN + half * 32)
+            dst = self._rows((got if received else sent) * HALF + half * QTR)
             src = dst
-        return remote(src, dst, self.ss.at[i], self.rs.at[i], dev)
+        return remote(src, dst, self.ss, self.rs.at[i], dev)
 
     def send(self, *idx):
         for i in idx:
@@ -144,7 +148,7 @@
             self._copy(i, True).wait_recv()
 
     def s0(self):
-        self.send(0, 1, 4, 5, 2, 3)
+        self.send(0, 1, 2, 3, 4, 5)
 
     def s1(self):
         self.recv(0)
@@ -168,8 +172,8 @@
         self.recv(4, 5, 7, 9, 10, 11, 12, 13)
 
     def drain(self):
-        for i in range(14):
-            self._copy(i, False).wait_send()
+        sent = self.buf.at[pl.ds(0, 14 * QTR)]
+        remote(sent, sent, self.ss, self.rs.at[0], self.t[0][3]).wait_send()
 
 
 class DpGather:
@@ -199,22 +203,22 @@
             ((x2, o, c), (x2, o, g), 0, r, core),
         ]
 
-    def _copy(self, i, received, src=None):
+    def _copy(self, i, received):
         sent, got, first, n, to = self.t[i]
         sx, sh, sc = got if received else sent
         ref = self.buf.at[sc, sx * 2 + sh, pl.ds(first, n)]
-        return remote(ref if src is None else src, ref, self.ss.at[i], self.rs.at[i], to)
-
-    def send(self, *idx, src=None):
+        return remote(ref, ref, self.ss.at[i // 10], self.rs.at[i], to)
+
+    def send(self, *idx):
         for i in idx:
-            self._copy(i, False, src).start()
+            self._copy(i, False).start()
 
     def recv(self, *idx):
         for i in idx:
             self._copy(i, True).wait_recv()
 
-    def s0(self, src=None):
-        self.send(1, 2, 3, 0, src=src)
+    def s0(self):
+        self.send(1, 2, 3, 0)
 
     def fwd(self, *ks):
         for k in ks:
@@ -236,8 +240,9 @@
             self.recv(k + 9 if k else 0)
 
     def drain(self):
-        for i in range(17):
-            self._copy(i, False).wait_send()
+        for i, n in enumerate((8, 7)):
+            sent = self.buf.at[0, pl.ds(0, n)]
+            remote(sent, sent, self.ss.at[i], self.rs.at[0], self.t[0][4]).wait_send()
 
 
 class RingReduce:
@@ -259,7 +264,7 @@
             (lambda: p.at[self.rd * 2 + 1], lambda: self.near.at[k, 3], self.dn),
             (lambda: self.ysend.at[k], lambda: self.yrecv.at[k], self.mate),
         ][i]
-        return remote(src(), dst(), self.ss.at[k, i], self.rs.at[k, i], to)
+        return remote(src(), dst(), self.ss.at[i], self.rs.at[k, (0, 1, 2, 2, 2, 2, 3)[i]], to)
 
     def stage1(self, k):
         for i in range(4):
@@ -273,8 +278,8 @@
             self._copy(4 + i, k).start()
 
     def stage3(self, k):
-        for i in (2, 3, 4, 5):
-            self._copy(i, k).wait_recv()
+        near = self.near.at[k]
+        remote(near, near, self.ss.at[2], self.rs.at[k, 2], self.up).wait_recv()
         p = self.part(k)
 
         def total(pair):
@@ -292,13 +297,9 @@
         self._copy(6, k).wait_recv()
         return self.yrecv[k].astype(F32)
 
-    def drain(self, n):
-        def body(k, _):
-            for i in range(7):
-                self._copy(i, k).wait_send()
-            return 0
-
-        lax.fori_loop(0, n, body, 0)
+    def drain(self):
+        for i in range(7):
+            remote(self.ysend, self.ysend, self.ss.at[i], self.rs.at[0, 3], self.up).wait_send()
 
 
 class ColumnReduce:
@@ -309,7 +310,7 @@
         self.up, self.dn, self.a, self.b = up, dn, mate_a, mate_b
 
     def _copy(self, i, k):
-        lo, hi = pl.ds(0, 32), pl.ds(32, 32)
+        lo, hi = pl.ds(0, QTR), pl.ds(QTR, QTR)
         src, dst, to = [
             (lambda: self.part.at[k, pl.ds(4, 2)], lambda: self.side.at[k, pl.ds(0, 2)], self.a),
             (lambda: self.part.at[k, pl.ds(6, 2)], lambda: self.side.at[k, pl.ds(2, 2)], self.b),
@@ -320,18 +321,19 @@
             (lambda: self.part.at[k, self.zu, lo], lambda: self.near.at[k, 0, lo], self.up),
             (lambda: self.part.at[k, self.zd, hi], lambda: self.near.at[k, 1, hi], self.dn),
         ][i]
-        return remote(src(), dst(), self.ss.at[k, i], self.rs.at[k, i], to)
+        return remote(src(), dst(), self.ss.at[i], self.rs.at[k, (0, 0, 1, 2, 3, 3, 3, 3)[i]], to)
 
     def stage1(self, k):
         self._copy(0, k).start()
         self._copy(1, k).start()
 
     def stage2(self, k):
+        side = self.side.at[k]
+        remote(side, side, self.ss.at[0], self.rs.at[k, 0], self.a).wait_recv()
         for i in range(2):
-            self._copy(i, k).wait_recv()
-            rows = pl.ds(32 * i, 32)
+            rows = pl.ds(QTR * i, QTR)
             for zz in range(4):
-                got = self.side[k, 2 * i + zz // 2, pl.ds(32 * (zz % 2), 32)]
+                got = self.side[k, 2 * i + zz // 2, pl.ds(QTR * (zz % 2), QTR)]
                 self.part[k, zz, rows] = (
                     self.part[k, zz, rows].astype(F32) + got.astype(F32)
                 ).astype(BF)
@@ -341,28 +343,25 @@
     def stage3(self, k):
         for i, blk in ((0, self.zu), (1, self.zd)):
             self._copy(2 + i, k).wait_recv()
-            rows = pl.ds(32 * i, 32)
+            rows = pl.ds(QTR * i, QTR)
             self.part[k, blk, rows] = (
-                self.part[k, blk, rows].astype(F32) + self.far[k, i, pl.ds(0, 32)].astype(F32)
+                self.part[k, blk, rows].astype(F32) + self.far[k, i, pl.ds(0, QTR)].astype(F32)
             ).astype(BF)
             self._copy(6 + i, k).start()
 
     def stage4(self, k):
-        for i in range(4, 8):
-            self._copy(i, k).wait_recv()
+        near = self.near.at[k]
+        remote(near, near, self.ss.at[4], self.rs.at[k, 3], self.up).wait_recv()
         return (
             self.part[k, self.z].astype(F32)
             + self.near[k, 0].astype(F32)
             + self.near[k, 1].astype(F32)
         )
 
-    def drain(self, n):
-        def body(k, _):
-            for i in range(8):
-                self._copy(i, k).wait_send()
-            return 0
-
-        lax.fori_loop(0, n, body, 0)
+    def drain(self):
+        for i in range(8):
+            sent = self.side.at[:, pl.ds(0, 2)] if i < 2 else self.far.at[:, 0, pl.ds(0, QTR)]
+            remote(sent, sent, self.ss.at[i], self.rs.at[0, 3], self.up).wait_send()
 
 
 def kernel(
@@ -399,29 +398,35 @@
     kvw[p.c, own_chip, 0:HD, :] = key_w[...]
     kvw[p.c, own_chip, HD : 2 * HD, :] = value_w[...]
     own = pl.multiple_of(p.tn * OWN, OWN)
-    own_z = pl.multiple_of(p.z * OWN, OWN)
 
     def normed(src, gain, dst, at):
         def body(i, _):
             r = pl.multiple_of(i * 16, 16)
             v = src[pl.ds(r, 16), :].astype(F32)
             s = lax.rsqrt(jnp.mean(v * v, axis=-1, keepdims=True) + 1e-06)
-            dst[pl.ds(pl.multiple_of(at + r, 16), 16), :] = (v * s * gain[...]).astype(BF)
+            dst[pl.ds(pl.multiple_of(at(i), 16), 16), :] = (v * s * gain[...]).astype(BF)
             return 0
 
         lax.fori_loop(0, OWN // 16, body, 0)
 
     kv = DpGather(p, kvw, kv_ss, kv_rs, 2 * HD)
     down = DpGather(p, down_all, dn_ss, dn_rs, FFL // WR)
-    res = ColumnGather(p, res_g, res_ss, res_rs, z_up, z_dn, mate, mate_b)
+    def column_gather(buf, ss, rs):
+        return [
+            ColumnGather(p, buf, b * TH, ss.at[b], rs.at[b], z_up, z_dn, mate, mate_b)
+            for b in range(2)
+        ]
+
+    res = column_gather(res_g, res_ss, res_rs)
     stm = TensorGather(p, str_g, str_ss, str_rs)
-    ffn = ColumnGather(p, ffn_g, ffn_ss, ffn_rs, z_up, z_dn, mate, mate_b)
+    ffn = column_gather(ffn_g, ffn_ss, ffn_rs)
 
     pl.semaphore_wait(barrier, 8)
     kv.s0()
-    normed(residual, ffn_gain, res_g, own_z)
-    res.s0()
-    normed(stream, final_gain, str_g, own)
+    normed(residual, ffn_gain, res_g, lambda i: (i // 2) * TH + p.z * HALF + (i % 2) * 16)
+    res[0].s0()
+    res[1].s0()
+    normed(stream, final_gain, str_g, lambda i: own + i * 16)
 
     s_t = dot(keys[...], queries[...], NT)
     e_t = jnp.exp(s_t - jnp.max(s_t, axis=0, keepdims=True))
@@ -454,12 +459,10 @@
     )
 
     def chunk_of(k):
-        if isinstance(k, int):
-            return [
-                p.x * 2 + p.h, p.x * 2 + 1 - p.h, p.xd * 2 + p.h, p.xu * 2 + p.h,
-                p.xd * 2 + 1 - p.h, p.xu * 2 + 1 - p.h, p.x2 * 2 + p.h, p.x2 * 2 + 1 - p.h,
-            ][k]
-        raise TypeError
+        return [
+            p.x * 2 + p.h, p.x * 2 + 1 - p.h, p.xd * 2 + p.h, p.xu * 2 + p.h,
+            p.xd * 2 + 1 - p.h, p.xu * 2 + 1 - p.h, p.x2 * 2 + p.h, p.x2 * 2 + 1 - p.h,
+        ][ARRIVAL[k]]
 
     def start_down():
         down_own.wait()
@@ -470,62 +473,77 @@
         for cc in range(2):
             blk = dot(kvg[:, 0:HD], kvw[cc, chip, 0:HD, :], NT)
             blk = blk + dot(kvg[:, HD : 2 * HD], kvw[cc, chip, HD : 2 * HD, :], NT)
-            part[k, :, :, cc * HD : (cc + 1) * HD] = blk.astype(BF).reshape(8, OWN, HD)
-
-    lag = 4
+            blk = blk.astype(BF).reshape(8, 2, HALF, HD)
+            for b in range(2):
+                part[b * NCH + k, :, :, cc * HD : (cc + 1) * HD] = blk[:, b]
+
+    def cols(k):
+        return pl.ds(pl.multiple_of(chunk_of(k) * CW, CW), CW)
+
+    def stream_back(b):
+        rows = slice(b * HALF, (b + 1) * HALF)
+        sq = jnp.zeros((HALF, 1), F32)
+        ip = jnp.zeros((HALF, 1), F32)
+        for k in range(NCH):
+            v = stream[rows, cols(k)].astype(F32)
+            sq = sq + jnp.sum(v * v, axis=-1, keepdims=True)
+            ip = ip + jnp.sum(
+                acc[b * NCH + k] * final_gain[:, cols(k)] * v, axis=-1, keepdims=True
+            )
+        scale = lax.rsqrt(sq * (1.0 / D) + 1e-06)
+        mix = scale * scale * scale * (ip * (1.0 / D))
+        at = pl.ds(pl.multiple_of(b * TH + p.z * HALF, HALF), HALF)
+        for k in range(NCH):
+            v = stream[rows, cols(k)].astype(F32)
+            grad = scale * (acc[b * NCH + k] * final_gain[:, cols(k)]) - v * mix
+            sgrad[rows, cols(k)] = grad
+            ffn_g[at, cols(k)] = grad.astype(BF)
+        ffn[b].s0()
+
+    lag = LE
+    F0 = NCH - 1 + 3 * lag
     before = {
-        1: lambda: kv.fwd(1),
-        2: lambda: kv.fwd(2, 3),
-        4: lambda: kv.fwd(4, 5),
-        6: lambda: kv.fwd(6),
+        1: lambda: kv.fwd(2, 3),
+        3: lambda: kv.fwd(6),
+        4: lambda: kv.fwd(1),
+        5: lambda: kv.fwd(4, 5),
         7: lambda: kv.fwd(7),
     }
-    after = {
-        2: res.s1,
-        4: start_down,
-        5: res.s2,
-        7: res.s3,
-        9: lambda: down.fwd(1),
-        11: lambda: down.fwd(2, 3),
-    }
-    for k in range(NCH + 2 + lag):
+    after = [
+        (2, res[0].s1), (3, res[1].s1), (5, start_down), (6, res[0].s2), (7, res[1].s2),
+        (8, res[0].s3), (9, res[1].s3), (11, lambda: down.fwd(2, 3)), (12, lambda: down.fwd(1)),
+        (F0 + 3, ffn[0].s1), (F0 + 4, lambda: down.fwd(4, 5)), (F0 + 5, ffn[0].s2),
+        (F0 + 6, ffn[0].s3), (F0 + 7, lambda: down.fwd(6, 7)),
+    ]
+
+    def flush(k):
+        while after and after[0][0] <= k:
+            after.pop(0)[1]()
+
+    for k in range(NQ + 3 * lag):
         if k in before:
             before[k]()
         if k < NCH:
-            kv.done(k)
+            kv.done(ARRIVAL[k])
             enc_compute(k)
+        if k < NQ:
             enc_rs.stage1(k)
-        if k in after:
-            after[k]()
-        if 0 <= k - lag < NCH:
+        flush(k)
+        if 0 <= k - lag < NQ:
             enc_rs.stage2(k - lag)
-        if 0 <= k - lag - 1 < NCH:
-            acc[k - lag - 1] = enc_rs.stage3(k - lag - 1)
-        if 0 <= k - lag - 2 < NCH:
-            acc[k - lag - 2] = acc[k - lag - 2] + enc_rs.stage4(k - lag - 2)
-
-    def cols(k):
-        start = chunk_of(k) * CW
-        return pl.ds(pl.multiple_of(start, CW), CW)
-
-    sq = jnp.zeros((OWN, 1), F32)
-    ip = jnp.zeros((OWN, 1), F32)
-    for k in range(NCH):
-        v = stream[:, cols(k)].astype(F32)
-        sq = sq + jnp.sum(v * v, axis=-1, keepdims=True)
-        ip = ip + jnp.sum(acc[k] * final_gain[:, cols(k)] * v, axis=-1, keepdims=True)
-    scale = lax.rsqrt(sq * (1.0 / D) + 1e-06)
-    mix = scale * scale * scale * (ip * (1.0 / D))
-    for k in range(NCH):
-        v = stream[:, cols(k)].astype(F32)
-        grad = scale * (acc[k] * final_gain[:, cols(k)]) - v * mix
-        sgrad[:, cols(k)] = grad
-        ffn_g[pl.ds(own_z, OWN), cols(k)] = grad.astype(BF)
-    ffn.s0()
+        if 0 <= k - 2 * lag < NQ:
+            acc[k - 2 * lag] = enc_rs.stage3(k - 2 * lag)
+        if 0 <= k - 3 * lag < NQ:
+            acc[k - 3 * lag] = acc[k - 3 * lag] + enc_rs.stage4(k - 3 * lag)
+        if k - 3 * lag == NCH - 1:
+            stream_back(0)
+    stream_back(1)
+    stm.s0()
 
     gate_load.wait()
     up_load.wait()
-    res.s4()
+    res[0].s4()
+    res[1].s4()
 
     def gate_tile(j):
         c0 = pl.ds(pl.multiple_of(j * HD, HD), HD)
@@ -539,15 +557,13 @@
         lax.fori_loop(lo, hi, lambda j, _: (gate_tile(j), 0)[1], 0)
 
     gate_tiles(0, 1)
-    down.fwd(4, 5)
-    ffn.s1()
-    stm.s0()
+    flush(99)
+    ffn[1].s1()
     gate_tiles(1, 2)
-    ffn.s2()
+    ffn[1].s2()
+    stm.s1()
     gate_tiles(2, 3)
-    down.fwd(6, 7)
-    ffn.s3()
-    stm.s1()
+    ffn[1].s3()
     gate_tiles(3, 4)
     down.done(*range(8))
 
@@ -568,40 +584,58 @@
     def core_copy(k):
         rows = pl.ds(pl.multiple_of(k * WR, WR), WR)
         return remote(
-            kvw.at[1 - p.c, :, rows, :], crecv.at[k], cs_ss.at[k], cs_rs.at[k], core
+            kvw.at[1 - p.c, :, rows, :], crecv.at[k], cs_ss, cs_rs.at[k], core
         )
 
-    enc_rs.drain(NCH)
+    enc_rs.drain()
     kv.drain()
-    stm.s2()
-    ffn.s4()
-
-    def hidden_tile(j, _):
-        @pl.when(j < 3)
-        def _():
-            down_load(j + 1).start()
-
-        down_load(j).wait()
-        s = j % 2
-        hid = jnp.zeros((TOK, HD), F32)
-        for i in range(16):
-            hid = hid + dot(ffn_g[:, i * HD : (i + 1) * HD], down_v[s, i % 2, i // 2].reshape(HD, HD), NT)
-        c0 = pl.ds(pl.multiple_of(j * HD, HD), HD)
-        ggrad[:, c0] = (hid * coef_a[:, c0].astype(F32)).astype(BF)
-        ugrad[:, c0] = (hid * coef_b[:, c0].astype(F32)).astype(BF)
-        return 0
-
-    lax.fori_loop(0, 4, hidden_tile, 0)
+    ffn[0].s4()
+
+    def hidden(b):
+        rows = slice(b * TH, (b + 1) * TH)
+
+        def tile(j, _):
+            @pl.when(j < 3)
+            def _():
+                down_load(j + 1).start()
+
+            down_load(j).wait()
+            s = j % 2
+            hid = jnp.zeros((TH, HD), F32)
+            for i in range(16):
+                hid = hid + dot(
+                    ffn_g[rows, i * HD : (i + 1) * HD],
+                    down_v[s, i % 2, i // 2].reshape(HD, HD), NT,
+                )
+            c0 = pl.ds(pl.multiple_of(j * HD, HD), HD)
+            ggrad[rows, c0] = (hid * coef_a[rows, c0].astype(F32)).astype(BF)
+            ugrad[rows, c0] = (hid * coef_b[rows, c0].astype(F32)).astype(BF)
+            return 0
+
+        lax.fori_loop(0, 4, tile, 0)
+
+    hidden(0)
+    down_load(0).start()
 
     def in_step(k, _):
-        @pl.when(k < NCH)
-        def _():
-            rows = pl.ds(pl.multiple_of(k * CW, CW), CW)
-            blk = dot(ggrad[...], gate_v[rows, :], NT) + dot(ugrad[...], up_v[rows, :], NT)
-            part[k] = blk.astype(BF).reshape(8, OWN, CW)
+        @pl.when(k == NCH)
+        def _():
+            ffn[1].s4()
+            hidden(1)
+
+        @pl.when(k < NQ)
+        def _():
+            rows = pl.ds(pl.multiple_of((k % NCH) * CW, CW), CW)
+            toks = pl.ds(pl.multiple_of((k // NCH) * TH, TH), TH)
+            blk = dot(ggrad[toks, :], gate_v[rows, :], NT) + dot(ugrad[toks, :], up_v[rows, :], NT)
+            part[k] = blk.astype(BF).reshape(8, HALF, CW)
             in_rs.stage1(k)
 
-        @pl.when(k == 1)
+        @pl.when(k == S2)
+        def _():
+            stm.s2()
+
+        @pl.when(k == S3)
         def _():
             stm.s3()
 
@@ -621,60 +655,61 @@
             mine[...] = (mine[...].astype(F32) + crecv[w].astype(F32)).astype(BF)
             w_rs.stage1(w)
 
-        @pl.when((k >= 1) & (k < NCH + 1))
-        def _():
-            in_rs.stage2(k - 1)
-
-        @pl.when((w >= 1) & (w < WCH + 1))
-        def _():
-            w_rs.stage2(w - 1)
-
-        @pl.when((k >= 2) & (k < NCH + 2))
-        def _():
-            in_rs.stage3(k - 2)
-
-        @pl.when((w >= 2) & (w < WCH + 2))
-        def _():
-            wacc[w - 2] = w_rs.stage3(w - 2)
-
-        @pl.when((k >= 3) & (k < NCH + 3))
-        def _():
-            acc[k - 3] = in_rs.stage4(k - 3)
-
-        @pl.when((w >= 3) & (w < WCH + 3))
-        def _():
-            wacc[w - 3] = wacc[w - 3] + w_rs.stage4(w - 3)
+        @pl.when((k >= 1 * LI) & (k < NQ + 1 * LI))
+        def _():
+            in_rs.stage2(k - LI)
+
+        @pl.when((w >= 1 * LW) & (w < WCH + 1 * LW))
+        def _():
+            w_rs.stage2(w - LW)
+
+        @pl.when((k >= 2 * LI) & (k < NQ + 2 * LI))
+        def _():
+            in_rs.stage3(k - 2 * LI)
+
+        @pl.when((w >= 2 * LW) & (w < WCH + 2 * LW))
+        def _():
+            wacc[w - 2 * LW] = w_rs.stage3(w - 2 * LW)
+
+        @pl.when((k >= 3 * LI) & (k < NQ + 3 * LI))
+        def _():
+            acc[k - 3 * LI] = in_rs.stage4(k - 3 * LI)
+
+        @pl.when((w >= 3 * LW) & (w < WCH + 3 * LW))
+        def _():
+            wacc[w - 3 * LW] = wacc[w - 3 * LW] + w_rs.stage4(w - 3 * LW)
 
         return 0
 
-    lax.fori_loop(0, max(NCH + 3, W0 + WCH + 4), in_step, 0)
+    lax.fori_loop(0, max(NQ + 3 * LI, W0 + 1 + WCH + 3 * LW), in_step, 0)
 
     for half in range(2):
         kwg_ref[:, half * WR : (half + 1) * WR] = wacc[half].T.astype(BF)
         vwg_ref[:, half * WR : (half + 1) * WR] = wacc[2 + half].T.astype(BF)
 
-    sq = jnp.zeros((OWN, 1), F32)
-    ip = jnp.zeros((OWN, 1), F32)
-    for k in range(NCH):
-        c0 = slice(k * CW, (k + 1) * CW)
-        v = residual[:, c0].astype(F32)
-        sq = sq + jnp.sum(v * v, axis=-1, keepdims=True)
-        ip = ip + jnp.sum(acc[k] * ffn_gain[:, c0] * v, axis=-1, keepdims=True)
-    scale = lax.rsqrt(sq * (1.0 / D) + 1e-06)
-    mix = scale * scale * scale * (ip * (1.0 / D))
-    for k in range(NCH):
-        c0 = slice(k * CW, (k + 1) * CW)
-        v = residual[:, c0].astype(F32)
-        out_ref[:, c0] = (
-            sgrad[:, c0] + scale * (acc[k] * ffn_gain[:, c0]) - v * mix
-        ).astype(BF)
-
-    for g in (res, stm, ffn, down):
+    for b in range(2):
+        rows = slice(b * HALF, (b + 1) * HALF)
+        sq = jnp.zeros((HALF, 1), F32)
+        ip = jnp.zeros((HALF, 1), F32)
+        for k in range(NCH):
+            c0 = slice(k * CW, (k + 1) * CW)
+            v = residual[rows, c0].astype(F32)
+            sq = sq + jnp.sum(v * v, axis=-1, keepdims=True)
+            ip = ip + jnp.sum(acc[b * NCH + k] * ffn_gain[:, c0] * v, axis=-1, keepdims=True)
+        scale = lax.rsqrt(sq * (1.0 / D) + 1e-06)
+        mix = scale * scale * scale * (ip * (1.0 / D))
+        for k in range(NCH):
+            c0 = slice(k * CW, (k + 1) * CW)
+            v = residual[rows, c0].astype(F32)
+            out_ref[rows, c0] = (
+                sgrad[rows, c0] + scale * (acc[b * NCH + k] * ffn_gain[:, c0]) - v * mix
+            ).astype(BF)
+
+    for g in (*res, stm, *ffn, down):
         g.drain()
-    in_rs.drain(NCH)
-    w_rs.drain(WCH)
-    for k in range(WCH):
-        core_copy(k).wait_send()
+    in_rs.drain()
+    w_rs.drain()
+    remote(crecv, crecv, cs_ss, cs_rs.at[0], core).wait_send()
 
 
 def place_results(*refs):
@@ -704,20 +739,20 @@
             v((2, 8, 2 * HD, HD), BF),
             v((D, FFL), BF), v((D, FFL), BF),
             v((2, 2, 8, 2, WR, HD), BF),
-            v((NCH, 8, OWN, CW), BF),
-            v((NCH, 2, OWN, CW), BF), v((NCH, 4, OWN, CW), BF),
-            v((NCH, OWN, CW), BF), v((NCH, OWN, CW), BF),
-            v((NCH, 2, OWN, CW), BF),
+            v((NQ, 8, HALF, CW), BF),
+            v((NQ, 2, HALF, CW), BF), v((NQ, 4, HALF, CW), BF),
+            v((NQ, HALF, CW), BF), v((NQ, HALF, CW), BF),
+            v((NQ, 2, HALF, CW), BF),
             v((TOK, FFL), BF), v((TOK, FFL), BF), v((TOK, FFL), BF), v((TOK, FFL), BF),
-            v((NCH, OWN, CW), F32), v((OWN, D), F32),
+            v((NQ, HALF, CW), F32), v((OWN, D), F32),
             v((TOK, 2 * HD), BF), v((2 * HD, TOK), BF),
             v((WCH, 8, WR, HD), BF),
             v((WCH, 2, WR, HD), BF), v((WCH, 4, WR, HD), BF),
             v((WCH, WR, HD), BF), v((WCH, WR, HD), BF), v((WCH, WR, HD), F32),
-            dma((14,)), dma((14,)), dma((9,)), dma((9,)), dma((14,)), dma((14,)),
-            dma((17,)), dma((17,)), dma((17,)), dma((17,)),
-            dma((NCH, 7)), dma((NCH, 7)), dma((NCH, 8)), dma((NCH, 8)),
-            dma((WCH, 7)), dma((WCH, 7)), dma((WCH,)), dma((WCH,)),
+            dma((2,)), dma((2, 14)), dma, dma((9,)), dma((2,)), dma((2, 14)),
+            dma((2,)), dma((17,)), dma((2,)), dma((17,)),
+            dma((7,)), dma((NQ, 4)), dma((8,)), dma((NQ, 4)),
+            dma((7,)), dma((WCH, 4)), dma, dma((WCH,)),
             dma((4,)), dma((2,)),
         ],
         compiler_params=pltpu.CompilerParams(

time: 167 us -> 159 us (0.952)
  Pallas kernels: 166 us -> 157 us
    pallas_call x1, Pallas kernels: 164 us -> 155 us  [local(): pl.pallas_call(kernel, out_shape=(sds((OWN, D), BF), sds((Q, HD), BF), sd...]
where the time goes in v3:
time: 159 us; the launch traced here: 158 us
  Pallas kernels  157 us (99%)
    pallas_call x1, Pallas kernels, local(): pl.pallas_call(kernel, out_shape=(sds((OWN, D), BF), sds((Q, HD), BF), sd...  155 us

profile of v3, /device:TPU:0, one launch (start us, length us, event | category | flops | bytes accessed | tf_op | source)
XLA Modules:
  0.0 157.9 jit_solution(5191452885868786138)
XLA Ops:
  0.6 155.2 %cross_ffn_backward.1 = (bf16[64,4096]{1,0:T(8,128)(2,1)}, bf16[256,256]{1,0:T(8,128)(2,1)}, bf16[256,256]{1,0:T(8,128)(2,1)}, bf16[256,256]{1,0:T(8,128)(2,1)}, bf16[2,8,8,128,256]{4,3,2,1,0:T(8,128)(2,1)}) custom-call(bf16[64,4096]{1,0:T(8,128)(2,1)} %stream.1, f32[1,4096]{1,0:T(1,128)} %bitcast.4, bf16[64,4096]{1,0:T(8,128)(2,1)} %residual.1, ...), custom_call_target="tpu_custom_call" | custom-call | tf_op jit(solution)/shard_map/cross_ffn_backward/pallas_call | solution.py:729
  155.8 2.1 %place_results.1 = (bf16[64,4096]{1,0:T(8,128)(2,1)}, bf16[256,256]{1,0:T(8,128)(2,1)}, bf16[256,256]{1,0:T(8,128)(2,1)}, bf16[256,256]{1,0:T(8,128)(2,1)}) custom-call(bf16[64,4096]{1,0:T(8,128)(2,1)} %get-tuple-element.8.refs_0_, bf16[256,256]{1,0:T(8,128)(2,1)} %get-tuple-element.9.refs_1_, bf16[256,256]{1,0:T(8,128)(2,1)} %get-tuple-element.10.refs_2_, ...), custom_call_target="tpu_custom_call" | custom-call | tf_op jit(solution)/shard_map/place_results/pallas_call | solution.py:767

commit v4 on v3

--- a/solution.py
+++ b/solution.py
@@ -14,9 +14,9 @@
 HALF, QTR = OWN // 2, OWN // 4
 WCH, WR = 4, 128
 ARRIVAL = (0, 2, 3, 6, 1, 4, 5, 7)
-LE, LI, LW = 5, 6, 4
-S2, S3 = 2, 6
-W0 = 11
+LE, LI, LW = 5, 7, 5
+S2, S3 = 1, 3
+W0 = 7
 
 NN = (((1,), (0,)), ((), ()))
 NT = (((1,), (1,)), ((), ()))
@@ -427,6 +427,7 @@
     res[0].s0()
     res[1].s0()
     normed(stream, final_gain, str_g, lambda i: own + i * 16)
+    stm.s0()
 
     s_t = dot(keys[...], queries[...], NT)
     e_t = jnp.exp(s_t - jnp.max(s_t, axis=0, keepdims=True))
@@ -538,7 +539,6 @@
         if k - 3 * lag == NCH - 1:
             stream_back(0)
     stream_back(1)
-    stm.s0()
 
     gate_load.wait()
     up_load.wait()

time: 159 us -> 154 us (0.969)
  Pallas kernels: 157 us -> 153 us
    pallas_call x1, Pallas kernels: 155 us -> 151 us  [local(): pl.pallas_call(kernel, out_shape=(sds((OWN, D), BF), sds((Q, HD), BF), sd...]
where the time goes in v4:
time: 154 us
  Pallas kernels  153 us (99%)
    pallas_call x1, Pallas kernels, local(): pl.pallas_call(kernel, out_shape=(sds((OWN, D), BF), sds((Q, HD), BF), sd...  151 us

profile of v4, /device:TPU:0, one launch (start us, length us, event | category | flops | bytes accessed | tf_op | source)
XLA Modules:
  0.0 153.7 jit_solution(12717409657422981458)
XLA Ops:
  0.6 150.9 %cross_ffn_backward.1 = (bf16[64,4096]{1,0:T(8,128)(2,1)}, bf16[256,256]{1,0:T(8,128)(2,1)}, bf16[256,256]{1,0:T(8,128)(2,1)}, bf16[256,256]{1,0:T(8,128)(2,1)}, bf16[2,8,8,128,256]{4,3,2,1,0:T(8,128)(2,1)}) custom-call(bf16[64,4096]{1,0:T(8,128)(2,1)} %stream.1, f32[1,4096]{1,0:T(1,128)} %bitcast.4, bf16[64,4096]{1,0:T(8,128)(2,1)} %residual.1, ...), custom_call_target="tpu_custom_call" | custom-call | tf_op jit(solution)/shard_map/cross_ffn_backward/pallas_call | solution.py:729
  151.6 2.1 %place_results.1 = (bf16[64,4096]{1,0:T(8,128)(2,1)}, bf16[256,256]{1,0:T(8,128)(2,1)}, bf16[256,256]{1,0:T(8,128)(2,1)}, bf16[256,256]{1,0:T(8,128)(2,1)}) custom-call(bf16[64,4096]{1,0:T(8,128)(2,1)} %get-tuple-element.8.refs_0_, bf16[256,256]{1,0:T(8,128)(2,1)} %get-tuple-element.9.refs_1_, bf16[256,256]{1,0:T(8,128)(2,1)} %get-tuple-element.10.refs_2_, ...), custom_call_target="tpu_custom_call" | custom-call | tf_op jit(solution)/shard_map/place_results/pallas_call | solution.py:767
